TPU v7x, 32 devices: a whole 2x2x4 slice. The times are simulated.
32 devices in a mesh: seq: 8 (over z, x), head: 4 (over y, core).
Axes of the slice: x: 2, y: 2, z: 4, core: 2. Of those that a mesh axis runs over, the one named last changes fastest.
Arguments:
- word_input: bfloat16 [4096, 512], P('seq'), may hold values from -6 to 6
- char_input: bfloat16 [4096, 16, 256], P('seq'), may hold values from -6 to 6
- char_count: int32 [4096], P('seq'), may hold values from 1 to 16
- document_ids: int32 [4096], P('seq'), may hold values from 0 to 2, as said below
- output_grad: bfloat16 [4096, 512], P('seq'), may hold values from -6 to 6
- char_gain: float32 [256], replicated, may hold values from 0.5 to 1.5
- char_proj: bfloat16 [3, 256, 256], P(None, None, 'head'), may hold values from -0.375 to 0.375
- char_out: bfloat16 [256, 256], P('head'), may hold values from -1.5 to 1.5
- pool_gain: float32 [256], replicated, may hold values from 0.5 to 1.5
- pool_proj: bfloat16 [256, 512], replicated, may hold values from -0.375 to 0.375
- attn_gain: float32 [512], replicated, may hold values from 0.5 to 1.5
- attn_proj: bfloat16 [3, 512, 512], P(None, None, 'head'), may hold values from -0.25 to 0.25
- attn_out: bfloat16 [512, 512], P('head'), may hold values from -6 to 6
- ffn_gain: float32 [512], replicated, may hold values from 0.5 to 1.5
- ffn_up: bfloat16 [512, 2048], P(None, 'head'), may hold values from -0.25 to 0.25
- ffn_down: bfloat16 [2048, 512], P('head'), may hold values from -0.5 to 0.5
Outputs:
- layer_out: bfloat16 [4096, 512], P('seq')
- grad_words: bfloat16 [4096, 512], P('seq')
- grad_chars: bfloat16 [4096, 16, 256], P(('seq', 'head'))
- grad_char_gain: float32 [256], replicated
- grad_char_proj: float32 [3, 256, 256], P(None, None, 'head')
- grad_char_out: float32 [256, 256], P('head')
- grad_pool_gain: float32 [256], replicated
- grad_pool_proj: float32 [256, 512], replicated
- grad_attn_gain: float32 [512], replicated
- grad_attn_proj: float32 [3, 512, 512], P(None, None, 'head')
- grad_attn_out: float32 [512, 512], P('head')
- grad_ffn_gain: float32 [512], replicated
- grad_ffn_up: float32 [512, 2048], P(None, 'head')
- grad_ffn_down: float32 [2048, 512], P('head')
Inputs may be any that keep to these rules, and one draw needn't show every extreme that they name: `document_ids`: document numbers begin at 0 with the first word, never fall, and rise by at most one from a word to the next; the sequence holds three documents.
All inputs are finite; a program needn't handle non-finite values.
Results may differ from a plain program's by a relative error of at most 0.024.
Values may be sent and summed in bfloat16 or wider, within the bound.
A program may use at most 320 MiB of HBM per device.

v0:
```python
import jax
import jax.numpy as jnp
from jax import lax
from jax.sharding import PartitionSpec as P

D = 512
HEADS = 8
CD = 256
CHEADS = 4


EPSILON = 1e-06
NEGATIVE = -1e30


def rms_forward(values, gain_vec):
    factor = lax.rsqrt(jnp.mean(values * values, axis=-1, keepdims=True) + EPSILON)
    normal = values * factor
    return (normal * gain_vec, normal, factor)


def rms_backward(upstream, normal, factor, gain_vec):
    scaled = upstream * gain_vec
    centre_term = jnp.mean(scaled * normal, axis=-1, keepdims=True)
    gain_grad = jnp.sum((upstream * normal).reshape(-1, normal.shape[-1]), axis=0)
    return (factor * (scaled - normal * centre_term), gain_grad)


def char_attention(normed_low, projection, char_valid, char_size):
    word_count, letters = (normed_low.shape[0], normed_low.shape[1])
    head_count = projection.shape[2] // char_size
    mapped = jnp.einsum("wlc,sce->swle", normed_low, projection, preferred_element_type=jnp.float32)
    mapped = mapped.astype(jnp.bfloat16).reshape(3, word_count, letters, head_count, char_size)
    scores = jnp.einsum(
        "wqhd,wkhd->whqk", mapped[0], mapped[1], preferred_element_type=jnp.float32
    ) * char_size ** (-0.5)
    scores = jnp.where(char_valid[:, None, None, :], scores, NEGATIVE)
    row_peak = jnp.max(scores, axis=-1, keepdims=True)
    raised = jnp.exp(scores - row_peak)
    return (mapped, raised / jnp.sum(raised, axis=-1, keepdims=True))


def char_front(char_rows, count_rows, char_gain, projection, char_size):
    word_count, letters = (char_rows.shape[0], char_rows.shape[1])
    char_valid = jnp.arange(letters, dtype=jnp.int32)[None, :] < count_rows[:, None]
    char_share = char_valid.astype(jnp.float32) / count_rows.astype(jnp.float32)[:, None]
    char_values = char_rows.astype(jnp.float32)
    char_normed, char_unit, char_factor = rms_forward(char_values, char_gain)
    char_low = char_normed.astype(jnp.bfloat16)
    char_mapped, char_weights = char_attention(char_low, projection, char_valid, char_size)
    char_mixed = jnp.einsum(
        "whqk,wkhd->wqhd",
        char_weights.astype(jnp.bfloat16),
        char_mapped[2],
        preferred_element_type=jnp.float32,
    )
    pooled_low = (
        jnp.sum(char_mixed * char_share[:, :, None, None], axis=1)
        .reshape(word_count, projection.shape[2])
        .astype(jnp.bfloat16)
    )
    mean_chars = jnp.sum(char_values * char_share[:, :, None], axis=1)
    return (char_valid, char_share, char_unit, char_factor, char_low, pooled_low, mean_chars)


def char_rear(
    summary_low, char_low, char_valid, char_share, projection, out_matrix, pooled_low, char_size
):
    word_count, letters = (char_low.shape[0], char_low.shape[1])
    char_width = projection.shape[2]
    char_scale = char_size ** (-0.5)
    grad_out_term = jnp.einsum(
        "we,wc->ec", pooled_low, summary_low, preferred_element_type=jnp.float32
    )
    grad_pooled = jnp.einsum(
        "wc,ec->we", summary_low, out_matrix, preferred_element_type=jnp.float32
    )
    grad_pooled = grad_pooled.reshape(word_count, 1, char_width // char_size, char_size)
    grad_char_mixed = (grad_pooled * char_share[:, :, None, None]).astype(jnp.bfloat16)
    char_again, weights_again = char_attention(char_low, projection, char_valid, char_size)
    char_dweights = jnp.einsum(
        "wqhd,wkhd->whqk", grad_char_mixed, char_again[2], preferred_element_type=jnp.float32
    )
    char_inner = jnp.sum(weights_again * char_dweights, axis=-1, keepdims=True)
    char_dscores = (weights_again * (char_dweights - char_inner)).astype(jnp.bfloat16)
    grad_char_query = (
        jnp.einsum(
            "whqk,wkhd->wqhd", char_dscores, char_again[1], preferred_element_type=jnp.float32
        )
        * char_scale
    ).astype(jnp.bfloat16)
    grad_char_key = (
        jnp.einsum(
            "whqk,wqhd->wkhd", char_dscores, char_again[0], preferred_element_type=jnp.float32
        )
        * char_scale
    ).astype(jnp.bfloat16)
    grad_char_value = jnp.einsum(
        "whqk,wqhd->wkhd",
        weights_again.astype(jnp.bfloat16),
        grad_char_mixed,
        preferred_element_type=jnp.float32,
    ).astype(jnp.bfloat16)
    char_grads = jnp.stack([grad_char_query, grad_char_key, grad_char_value]).reshape(
        3, word_count, letters, char_width
    )
    grad_proj_term = jnp.einsum(
        "wlc,swle->sce", char_low, char_grads, preferred_element_type=jnp.float32
    )
    upstream = jnp.einsum(
        "swle,sce->wlc", char_grads, projection, preferred_element_type=jnp.float32
    )
    return (grad_out_term, grad_proj_term, upstream)


def word_scores(query_rows, key_rows, query_pos, query_doc, key_pos, key_doc, head_size):
    head_count = query_rows.shape[1] // head_size
    query_split = query_rows.reshape(query_rows.shape[0], head_count, head_size)
    key_split = key_rows.reshape(key_rows.shape[0], head_count, head_size)
    scores = jnp.einsum(
        "qhd,khd->hqk", query_split, key_split, preferred_element_type=jnp.float32
    ) * head_size ** (-0.5)
    allowed = (key_pos[None, :] <= query_pos[:, None]) & (key_doc[None, :] == query_doc[:, None])
    return (scores, allowed[None])


def grad_block(
    query_rows,
    grad_rows,
    row_lse,
    row_delta,
    query_pos,
    query_doc,
    key_rows,
    value_rows,
    key_pos,
    key_doc,
    head_size,
):
    scores, allowed = word_scores(
        query_rows, key_rows, query_pos, query_doc, key_pos, key_doc, head_size
    )
    weights = jnp.where(allowed, jnp.exp(scores - row_lse[:, :, None]), 0.0)
    head_count = query_rows.shape[1] // head_size
    grad_split = grad_rows.reshape(grad_rows.shape[0], head_count, head_size)
    value_split = value_rows.reshape(value_rows.shape[0], head_count, head_size)
    dweights = jnp.einsum(
        "qhd,khd->hqk", grad_split, value_split, preferred_element_type=jnp.float32
    )
    dscores = (weights * (dweights - row_delta[:, :, None])).astype(jnp.bfloat16)
    return (weights.astype(jnp.bfloat16), dscores)


def keep_same(running):
    return running


def per_device(
    word_input,
    char_input,
    char_count,
    document_ids,
    output_grad,
    char_gain,
    char_proj,
    char_out,
    pool_gain,
    pool_proj,
    attn_gain,
    attn_proj,
    attn_out,
    ffn_gain,
    ffn_up,
    ffn_down,
):
    words_dev = word_input.shape[0]
    head_size = D // HEADS
    char_size = CD // CHEADS
    head_width = attn_proj.shape[2]
    local_heads = head_width // head_size
    rank_count = lax.axis_size("seq")
    first_row = lax.axis_index("seq") * words_dev
    all_words = words_dev * rank_count
    key_block = min(all_words, 4 * words_dev)
    block_count = all_words // key_block
    score_scale = head_size ** (-0.5)
    query_pos = first_row + jnp.arange(words_dev, dtype=jnp.int32)
    head_count_axis = lax.axis_size("head")
    quarter = words_dev // head_count_axis
    quarter_start = lax.axis_index("head") * quarter
    char_valid, char_share, char_unit, char_factor, char_low, pooled_low, mean_chars = char_front(
        char_input, char_count, char_gain, char_proj, char_size
    )
    summary = mean_chars + lax.psum(
        jnp.dot(pooled_low, char_out, preferred_element_type=jnp.float32), "head"
    )
    pool_normed, pool_unit, pool_factor = rms_forward(summary, pool_gain)
    pool_low = pool_normed.astype(jnp.bfloat16)
    hidden = word_input.astype(jnp.float32) + jnp.dot(
        pool_low, pool_proj, preferred_element_type=jnp.float32
    )
    attn_normed, attn_unit, attn_factor = rms_forward(hidden, attn_gain)
    attn_low = attn_normed.astype(jnp.bfloat16)
    mapped = jnp.einsum(
        "wc,sce->swe", attn_low, attn_proj, preferred_element_type=jnp.float32
    ).astype(jnp.bfloat16)
    query_low, key_low, value_low = (mapped[0], mapped[1], mapped[2])
    key_all, value_all, doc_wire = (
        lax.all_gather(key_low, "seq", axis=0, tiled=True),
        lax.all_gather(value_low, "seq", axis=0, tiled=True),
        lax.all_gather(document_ids.astype(jnp.bfloat16), "seq", axis=0, tiled=True),
    )
    doc_all = doc_wire.astype(jnp.int32)
    first_doc = document_ids[0]

    def key_needed(block_start, size):
        end_doc = lax.dynamic_index_in_dim(doc_all, block_start + size - 1, 0, keepdims=False)
        return (block_start < first_row + words_dev) & (end_doc >= first_doc)

    def key_slices(block_start, size):
        return (
            lax.dynamic_slice_in_dim(key_all, block_start, size, 0),
            lax.dynamic_slice_in_dim(value_all, block_start, size, 0),
            block_start + jnp.arange(size, dtype=jnp.int32),
            lax.dynamic_slice_in_dim(doc_all, block_start, size, 0),
        )

    def lse_step(block_index, running):
        block_start = block_index * key_block

        def lse_compute(running_in):
            key_rows, value_rows, key_pos, key_doc = key_slices(block_start, key_block)
            scores, allowed = word_scores(
                query_low, key_rows, query_pos, document_ids, key_pos, key_doc, head_size
            )
            new_peak = jnp.maximum(
                running_in[0], jnp.max(jnp.where(allowed, scores, NEGATIVE), axis=-1)
            )
            raised = jnp.where(allowed, jnp.exp(scores - new_peak[:, :, None]), 0.0)
            return (
                new_peak,
                running_in[1] * jnp.exp(running_in[0] - new_peak) + jnp.sum(raised, axis=-1),
            )

        return lax.cond(key_needed(block_start, key_block), lse_compute, keep_same, running)

    start_peak = jnp.full((local_heads, words_dev), NEGATIVE, jnp.float32)
    run_peak, run_total = lax.fori_loop(
        0, block_count, lse_step, (start_peak, jnp.zeros((local_heads, words_dev), jnp.float32))
    )
    row_lse = run_peak + jnp.log(run_total)

    def out_step(block_index, running):
        block_start = block_index * key_block

        def out_compute(running_in):
            key_rows, value_rows, key_pos, key_doc = key_slices(block_start, key_block)
            scores, allowed = word_scores(
                query_low, key_rows, query_pos, document_ids, key_pos, key_doc, head_size
            )
            weights_low = jnp.where(allowed, jnp.exp(scores - row_lse[:, :, None]), 0.0).astype(
                jnp.bfloat16
            )
            value_split = value_rows.reshape(key_block, local_heads, head_size)
            return running_in + jnp.einsum(
                "hqk,khd->qhd", weights_low, value_split, preferred_element_type=jnp.float32
            )

        return lax.cond(key_needed(block_start, key_block), out_compute, keep_same, running)

    attn_mixed = lax.fori_loop(
        0, block_count, out_step, jnp.zeros((words_dev, local_heads, head_size), jnp.float32)
    )
    mixed_low = attn_mixed.reshape(words_dev, head_width).astype(jnp.bfloat16)
    second = hidden + lax.psum(
        jnp.dot(mixed_low, attn_out, preferred_element_type=jnp.float32), "head"
    )
    ffn_normed, ffn_unit, ffn_factor = rms_forward(second, ffn_gain)
    ffn_low = ffn_normed.astype(jnp.bfloat16)
    upward = jnp.dot(ffn_low, ffn_up, preferred_element_type=jnp.float32)
    active, gelu_back = jax.vjp(jax.nn.gelu, upward)
    active_low = active.astype(jnp.bfloat16)
    layer_out = second + lax.psum(
        jnp.dot(active_low, ffn_down, preferred_element_type=jnp.float32), "head"
    )
    grad_ffn_down = jnp.einsum(
        "wf,wd->fd", active_low, output_grad, preferred_element_type=jnp.float32
    )
    grad_active = jnp.einsum("wd,fd->wf", output_grad, ffn_down, preferred_element_type=jnp.float32)
    grad_upward = gelu_back(grad_active)[0].astype(jnp.bfloat16)
    grad_ffn_up = jnp.einsum("wc,wf->cf", ffn_low, grad_upward, preferred_element_type=jnp.float32)
    ffn_sum = lax.psum(
        jnp.einsum("wf,cf->wc", grad_upward, ffn_up, preferred_element_type=jnp.float32), "head"
    )
    grad_second_norm, grad_ffn_gain = rms_backward(ffn_sum, ffn_unit, ffn_factor, ffn_gain)
    grad_second = output_grad.astype(jnp.float32) + grad_second_norm
    grad_branch = grad_second.astype(jnp.bfloat16)
    grad_attn_out = jnp.einsum(
        "we,wd->ed", mixed_low, grad_branch, preferred_element_type=jnp.float32
    )
    grad_low = jnp.einsum(
        "wd,ed->we", grad_branch, attn_out, preferred_element_type=jnp.float32
    ).astype(jnp.bfloat16)
    row_delta = jnp.sum(
        grad_low.astype(jnp.float32).reshape(words_dev, local_heads, head_size) * attn_mixed,
        axis=-1,
    ).T
    query_split = query_low.reshape(words_dev, local_heads, head_size)
    grad_split = grad_low.reshape(words_dev, local_heads, head_size)

    def query_grad_step(block_index, running):
        block_start = block_index * key_block

        def query_compute(running_in):
            key_rows, value_rows, key_pos, key_doc = key_slices(block_start, key_block)
            weights_low, dscores = grad_block(
                query_low,
                grad_low,
                row_lse,
                row_delta,
                query_pos,
                document_ids,
                key_rows,
                value_rows,
                key_pos,
                key_doc,
                head_size,
            )
            key_split = key_rows.reshape(key_block, local_heads, head_size)
            return running_in + jnp.einsum(
                "hqk,khd->qhd", dscores, key_split, preferred_element_type=jnp.float32
            )

        return lax.cond(key_needed(block_start, key_block), query_compute, keep_same, running)

    query_grad = lax.fori_loop(
        0, block_count, query_grad_step, jnp.zeros((words_dev, local_heads, head_size), jnp.float32)
    )
    grad_query_low = (query_grad.reshape(words_dev, head_width) * score_scale).astype(jnp.bfloat16)

    def one_step(step_index, partial_sum):
        key_start = step_index * key_block

        def one_compute(partial_in):
            key_rows, value_rows, key_pos, key_doc = key_slices(key_start, key_block)
            weights_low, dscores = grad_block(
                query_low,
                grad_low,
                row_lse,
                row_delta,
                query_pos,
                document_ids,
                key_rows,
                value_rows,
                key_pos,
                key_doc,
                head_size,
            )
            key_part = (
                jnp.einsum("hqk,qhd->khd", dscores, query_split, preferred_element_type=jnp.float32)
                * score_scale
            )
            value_part = jnp.einsum(
                "hqk,qhd->khd", weights_low, grad_split, preferred_element_type=jnp.float32
            )
            joined = jnp.concatenate(
                [
                    key_part.reshape(key_block, head_width),
                    value_part.reshape(key_block, head_width),
                ],
                axis=1,
            )
            return lax.dynamic_update_slice_in_dim(partial_in, joined, step_index * key_block, 0)

        return lax.cond(key_needed(key_start, key_block), one_compute, keep_same, partial_sum)

    joined_grad = lax.psum_scatter(
        lax.fori_loop(
            0,
            words_dev * lax.axis_size("seq") // key_block,
            one_step,
            jnp.zeros((words_dev * lax.axis_size("seq"), 2 * head_width), jnp.float32),
        ),
        "seq",
        scatter_dimension=0,
        tiled=True,
    )
    key_grad = joined_grad[:, :head_width]
    value_grad = joined_grad[:, head_width:]
    grad_mapped = jnp.stack(
        [grad_query_low, key_grad.astype(jnp.bfloat16), value_grad.astype(jnp.bfloat16)]
    )
    grad_attn_proj = jnp.einsum(
        "wc,swe->sce", attn_low, grad_mapped, preferred_element_type=jnp.float32
    )
    attn_sum = lax.psum(
        jnp.einsum("swe,sce->wc", grad_mapped, attn_proj, preferred_element_type=jnp.float32),
        "head",
    )
    grad_hidden_norm, grad_attn_gain = rms_backward(attn_sum, attn_unit, attn_factor, attn_gain)
    grad_hidden = grad_second + grad_hidden_norm
    grad_words = grad_hidden.astype(jnp.bfloat16)
    grad_pool_proj = jnp.einsum(
        "wc,wd->cd", pool_low, grad_words, preferred_element_type=jnp.float32
    )
    pool_upstream = jnp.einsum(
        "wd,cd->wc", grad_words, pool_proj, preferred_element_type=jnp.float32
    )
    grad_summary, grad_pool_gain = rms_backward(pool_upstream, pool_unit, pool_factor, pool_gain)
    grad_char_out, grad_char_proj, char_upstream = char_rear(
        grad_summary.astype(jnp.bfloat16),
        char_low,
        char_valid,
        char_share,
        char_proj,
        char_out,
        pooled_low,
        char_size,
    )
    char_sum = lax.psum(char_upstream, "head")
    grad_char_norm, grad_char_gain = rms_backward(char_sum, char_unit, char_factor, char_gain)
    grad_full = grad_char_norm + char_share[:, :, None] * grad_summary[:, None, :]
    grad_chars = lax.dynamic_slice_in_dim(grad_full, quarter_start, quarter, 0).astype(jnp.bfloat16)
    summed = lax.psum(
        (
            grad_char_gain,
            grad_char_proj,
            grad_char_out,
            grad_pool_gain,
            grad_pool_proj,
            grad_attn_gain,
            grad_attn_proj,
            grad_attn_out,
            grad_ffn_gain,
            grad_ffn_up,
            grad_ffn_down,
        ),
        "seq",
    )
    return (layer_out.astype(jnp.bfloat16), grad_words, grad_chars) + tuple(summed)


def solution(mesh):
    placed = (
        P("seq", None),
        P("seq", None, None),
        P("seq"),
        P("seq"),
        P("seq", None),
        P(),
        P(None, None, "head"),
        P("head", None),
        P(),
        P(),
        P(),
        P(None, None, "head"),
        P("head", None),
        P(),
        P(None, "head"),
        P("head", None),
    )
    return jax.shard_map(
        per_device,
        mesh=mesh,
        in_specs=placed,
        out_specs=(
            P("seq", None),
            P("seq", None),
            P(("seq", "head"), None, None),
            P(),
            P(None, None, "head"),
            P("head", None),
            P(),
            P(),
            P(),
            P(None, None, "head"),
            P("head", None),
            P(),
            P(None, "head"),
            P("head", None),
        ),
        check_vma=False,
    )
```

profile of v0, /device:TPU:12, one launch (start us, length us, event | category | flops | bytes accessed | tf_op | source)
XLA Modules:
  0.0 860.1 jit_solution(8416318899139988958)
XLA Ops:
  9.8 5.3 fusion.35
  15.2 3.9 convert_bitcast_fusion
  20.8 3.0 copy.106
  23.8 4.3 copy.107
  28.1 3.8 copy.108
  31.9 6.8 fusion.104
  38.7 4.8 fusion.42
  45.1 33.0 %all-reduce.10.cloned.1.call-done = f32[512,256]{1,0:T(8,128)} async-done(((f32[512,256]{1,0:T(8,128)}), f32[512,256]{1,0:T(8,128)}) %all-reduce.10.cloned.1.call-update) | async-done | bytes 524304 | tf_op jit(solution)/shard_map/psum | solution.py:194
  85.0 25.0 %all-gather.2 = bf16[8,1,512]{2,1,0:T(2,128)(2,1)S(1)} all-gather(bf16[1,1,512]{2,1,0:T(2,128)(2,1)S(1)} %reshape.565), channel_id=1, replica_groups=mesh['seq'=8,'head'=4] {'seq'}, dimensions={0}, use_global_device_ids=true | all-gather | bytes 9216 | tf_op jit(solution)/shard_map/all_gather | solution.py:211
  110.0 12.5 %all-gather.8.cloned.1.call-done = bf16[1,4096,128]{1,2,0:T(8,128)(2,1)} async-done(((bf16[1,512,128]{1,2,0:T(8,128)(2,1)}), bf16[1,4096,128]{1,2,0:T(8,128)(2,1)}) %all-gather.8.cloned.1.call-update) | async-done | bytes 1048592 | tf_op jit(solution)/shard_map/all_gather | solution.py:209
  122.6 11.4 %while.83 = (s32[]{:T(128)}, f32[2,512]{1,0:T(2,128)S(1)}, f32[2,512]{1,0:T(2,128)S(1)}, s32[]{:T(128)}, s32[4096]{0:T(1024)S(1)}, /*index=5*/s32[]{:T(128)}, s3...) while((s32[]{:T(128)}, f32[2,512]{1,0:T(2,128)S(1)}, ...), condition=%wide.region_13.14_spmd.clone, body=%wide.region_8.13_spmd.clone.sunk | while | flops 286265856 | bytes 21731728 | solution.py:248
  124.5 7.4 conditional.12
  134.5 29.1 %all-gather.6.cloned.1.call-done = bf16[1,4096,128]{1,2,0:T(8,128)(2,1)} async-done(((bf16[1,512,128]{1,2,0:T(8,128)(2,1)}), bf16[1,4096,128]{1,2,0:T(8,128)(2,1)}) %all-gather.6.cloned.1.call-update) | async-done | bytes 1048592 | tf_op jit(solution)/shard_map/all_gather | solution.py:210
  163.7 12.3 %while.84 = (s32[]{:T(128)}, f32[512,2,64]{0,2,1:T(8,128)S(1)}, s32[]{:T(128)}, s32[4096]{0:T(1024)S(1)}, s32[]{:T(128)}, /*index=5*/bf16[4096,128]{0,1:T(8,128)...) while((s32[]{:T(128)}, f32[512,2,64]{0,2,1:T(8,128)S(1)}, ...), condition=%wide.region_17.18_spmd.clone, body=%wide.region_14.17_spmd.clone.sunk | while | flops 548473344 | bytes 5953919 | solution.py:271
  165.6 8.3 conditional.13
  170.0 3.9 fusion.15
  178.3 2.6 fusion.110
  180.9 40.6 %all-reduce.12.cloned.1.call-done = f32[512,512]{0,1:T(8,128)} async-done(((f32[512,512]{0,1:T(8,128)}), f32[512,512]{0,1:T(8,128)}) %all-reduce.12.cloned.1.call-update) | async-done | bytes 1048592 | tf_op jit(solution)/shard_map/psum | solution.py:275
  223.1 3.6 fusion.77
  228.6 36.1 %all-reduce.14.cloned.1.call-done = f32[512,512]{0,1:T(8,128)} async-done(((f32[512,512]{0,1:T(8,128)}), f32[512,512]{0,1:T(8,128)}) %all-reduce.14.cloned.1.call-update) | async-done | bytes 1048592 | tf_op jit(solution)/shard_map/psum | solution.py:292
  269.8 2.4 multiply_reduce_fusion.12
  272.2 2.4 broadcast_in_dim.94
  274.7 30.2 %while.86 = (s32[]{:T(128)}, f32[4096,256]{0,1:T(8,128)}, s32[]{:T(128)}, s32[4096]{0:T(1024)S(1)}, s32[]{:T(128)}, /*index=5*/s32[512]{0:T(512)}, bf16[4096,128...) while((s32[]{:T(128)}, f32[4096,256]{0,1:T(8,128)}, ...), condition=%wide.region_31.32_spmd.clone, body=%wide.region_28.31_spmd.clone.sunk | while | flops 1098648064 | bytes 38353428 | solution.py:378
  276.5 26.5 %conditional.15 = (f32[4096,256]{0,1:T(8,128)}) conditional(s32[]{:T(128)} %convert_element_type.377, f32[4096,256]{0,1:T(8,128)} %get-tuple-element.2518, (s32[]{:T(128)}, s32[]{:T(128)}, s32[4096]{0:T(1024)S(1)}, s32[512]{0:T(512)}, bf16[4096,128]{0,1:T(8,128)(2,1)S(1)}, /*index=5*/bf16[1,512,128]{1,2,0:T(8,128)(2,1)S(1)}, f32[2,512]{1,0:T(2,128)}, ...), branch_computations={%region_29.29_spmd, %region_30.30_spmd} | conditional | flops 1098648064 | bytes 38350984 | solution.py:375
  276.6 3.2 compare_and_fusion.3
  279.9 4.6 fusion.108
  284.5 8.6 %convolution_multiply_fusion = f32[2,2048,64]{1,2,0:T(8,128)} fusion(bf16[512,2,64]{0,2,1:T(8,128)(2,1)S(1)} %get-tuple-element.1696, f32[2,2048,512]{2,1,0:T(8,128)} %fusion.108, bf16[2048,2,64]{0,2,1:T(8,128)(2,1)S(1)} %bitcast.244, bf16[512,2,64]{0,2,1:T(8,128)(2,1)S(1)} %get-tuple-element.1697, f32[2,512]{1,0:T(2,128)S(1)} %get-tuple-element.1695, ...), kind=kOutput, calls=%fused_computation.47 | convolution fusion | flops 549715968 | bytes 11280384 | tf_op jit(solution)/shard_map/while/body/eval_jaxpr/cond/branch_1_fun/hqk,qhd->khd/dot_general | solution.py:360
  293.1 6.8 fusion.26
  299.9 3.1 maximum_dynamic-update-slice_fusion
  304.9 5.6 copy.116
  311.5 2.8 fusion.101
  314.3 2.7 fusion.99
  317.1 19.1 %while.85 = (s32[]{:T(128)}, f32[512,2,64]{0,2,1:T(8,128)S(1)}, s32[]{:T(128)}, s32[4096]{0:T(1024)S(1)}, s32[]{:T(128)}, /*index=5*/bf16[4096,128]{0,1:T(8,128)...) while((s32[]{:T(128)}, f32[512,2,64]{0,2,1:T(8,128)S(1)}, ...), condition=%wide.region_27.28_spmd.clone, body=%wide.region_24.27_spmd.clone.sunk | while | flops 821103104 | bytes 23390624 | solution.py:336
  318.9 15.3 %conditional.14 = (f32[512,2,64]{0,2,1:T(8,128)S(1)}) conditional(s32[]{:T(128)} %convert_element_type.376, f32[512,2,64]{0,2,1:T(8,128)S(1)} %get-tuple-element.2576, (s32[]{:T(128)}, bf16[4096,128]{0,1:T(8,128)(2,1)S(1)}, s32[]{:T(128)}, s32[4096]{0:T(1024)S(1)}, s32[512]{0:T(512)}, /*index=5*/bf16[1,512,128]{1,2,0:T(8,128)(2,1)S(1)}, ...), branch_computations={%region_25.25_spmd, %region_26.26_spmd} | conditional | flops 821103104 | bytes 23388218 | solution.py:334
  319.0 3.2 compare_and_fusion.2
  322.3 4.6 fusion.107
  326.9 7.4 fusion.21
  336.4 89.8 %reduce-scatter.2.cloned.1.call-done = f32[512,256]{1,0:T(8,128)} async-done(((f32[4096,256]{1,0:T(8,128)}), f32[512,256]{1,0:T(8,128)}) %reduce-scatter.2.cloned.1.call-update) | async-done | bytes 524304 | tf_op jit(solution)/shard_map/reduce_scatter | solution.py:377
  427.3 2.5 convolution_bitcast_fusion
  432.5 32.6 %all-reduce.16.cloned.1.call-done = f32[512,512]{0,1:T(8,128)} async-done(((f32[512,512]{0,1:T(8,128)}), f32[512,512]{0,1:T(8,128)}) %all-reduce.16.cloned.1.call-update) | async-done | bytes 1048592 | tf_op jit(solution)/shard_map/psum | solution.py:396
  470.6 4.2 multiply_reduce_fusion.2
  483.6 2.7 copy-done.6
  486.3 5.7 fusion.66
  494.0 8.4 fusion.44
  504.2 138.7 %all-reduce.18.cloned.1.call-done = (f32[3,256,64]{1,2,0:T(8,128)}, f32[64,256]{1,0:T(8,128)}, f32[256,512]{1,0:T(8,128)}, f32[3,512,128]{1,2,0:T(8,128)}, f32[1...) async-done(((f32[3,256,64]{1,2,0:T(8,128)}, f32[64,256]{1,0:T(8,128)}, f32[256,512]{1,0:T(8,128)}, f32[3,512,128]{1,2,0:T(8,128)}, f32[128,512]{1,0:T(8,128)}, ...) | async-done | bytes 3932176 | tf_op jit(solution)/shard_map/psum | solution.py:424
  645.1 171.2 %all-reduce.20.cloned.1.call-done = (f32[512,512]{0,1:T(8,128)}, f32[512,16,256]{2,0,1:T(8,128)}) async-done(((f32[512,512]{0,1:T(8,128)}, f32[512,16,256]{2,0,1:T(8,128)}), (f32[512,512]{0,1:T(8,128)}, f32[512,16,256]{2,0,1:T(8,128)})) %all-reduce.20.cloned.1.call-update) | async-done | bytes 9437200 | tf_op jit(solution)/shard_map/psum | solution.py:283
  816.4 6.8 multiply_reduce_fusion
  827.1 19.4 %all-reduce = (f32[256]{0:T(256)}, f32[256]{0:T(256)}, f32[512]{0:T(512)}, f32[512]{0:T(512)}) all-reduce(f32[256]{0:T(256)S(1)} %get-tuple-element.1944, f32[256]{0:T(256)S(1)} %get-tuple-element.1952, f32[512]{0:T(512)S(1)} %get-tuple-element.1950, f32[512]{0:T(512)S(1)} %copy-done.60), channel_id=1, replica_groups=mesh['seq'=8,'head'=4] {'seq'}, use_global_device_ids=true, to_apply=%region_40.41 | all-reduce | flops 1536 | bytes 12288 | tf_op jit(solution)/shard_map/psum | solution.py:424
  (264 shorter events, 76.3 us)
Async XLA Ops:
  7.2 215.9 %copy-start = (bf16[512,512]{1,0:T(8,128)(2,1)S(1)}, bf16[512,512]{1,0:T(8,128)(2,1)}, u32[]{:S(2)}) copy-start(bf16[512,512]{1,0:T(8,128)(2,1)} %param.46) | copy-start | bytes 1572868
  7.2 8.0 copy-start.63
  7.2 8.0 copy-start.45
  7.2 70.9 %all-reduce.10.cloned.1.call-start = ((), (), s32[]{:S(2)}) async-start(), calls=%async_computation.1 | async-start | bytes 1048576 | tf_op jit(solution)/shard_map/psum | solution.py:194
  9.7 29.0 %copy-start.31 = (f32[512,16]{1,0:T(8,128)}, f32[512,16]{1,0:T(8,128)S(1)}, u32[]{:S(2)}) copy-start(f32[512,16]{1,0:T(8,128)S(1)} %convert_divide_fusion) | copy-start | bytes 98308
  9.8 9.3 %copy-start.39 = (f32[512,16]{0,1:T(8,128)}, f32[512,16]{0,1:T(8,128)S(1)}, u32[]{:S(2)}) copy-start(f32[512,16]{0,1:T(8,128)S(1)} %copy.105) | copy-start | bytes 98308
  9.8 5.4 copy-start.11
  23.8 14.9 %copy-start.15 = (bf16[512,16,64]{2,1,0:T(8,128)(2,1)}, bf16[512,16,64]{2,1,0:T(8,128)(2,1)S(1)}, u32[]{:S(2)}) copy-start(bf16[512,16,64]{2,1,0:T(8,128)(2,1)S(1)} %copy.106) | copy-start | bytes 3145732
  38.7 6.0 copy-start.33
  38.7 6.2 copy-start.24
  43.6 37.8 %copy-start.35 = (bf16[512,64]{1,0:T(8,128)(2,1)}, bf16[512,64]{1,0:T(8,128)(2,1)S(1)}, u32[]{:S(2)}) copy-start(bf16[512,64]{1,0:T(8,128)(2,1)S(1)} %fusion.42) | copy-start | bytes 196612
  43.6 35.8 %copy-start.58 = (f32[256]{0:T(256)S(1)}, f32[256]{0:T(256)}, u32[]{:S(2)}) copy-start(f32[256]{0:T(256)} %param.40) | copy-start | bytes 3076
  43.6 37.4 %copy-start.54 = (f32[512]{0:T(512)S(1)}, f32[512]{0:T(512)}, u32[]{:S(2)}) copy-start(f32[512]{0:T(512)} %param.42) | copy-start | bytes 6148
  44.6 77.9 %all-gather.8.cloned.1.call-start = ((), (), s32[]{:S(2)}) async-start(), calls=%async_computation.7 | async-start | bytes 1179648 | tf_op jit(solution)/shard_map/all_gather | solution.py:209
  79.3 43.2 %copy-start.48 = (f32[512]{0:T(512)}, f32[512]{0:T(512)S(1)}, u32[]{:S(2)}) copy-start(f32[512]{0:T(512)S(1)} %add_rsqrt_fusion.3) | copy-start | bytes 6148
  80.9 140.7 %copy-start.4 = (f32[512,512]{0,1:T(8,128)}, f32[512,512]{0,1:T(8,128)S(1)}, u32[]{:S(2)}) copy-start(f32[512,512]{0,1:T(8,128)S(1)} %get-tuple-element.2090) | copy-start | bytes 3145732
  80.9 41.6 %copy-start.50 = (f32[512]{0:T(512)}, f32[512]{0:T(512)S(1)}, u32[]{:S(2)}) copy-start(f32[512]{0:T(512)S(1)} %add_rsqrt_fusion.2) | copy-start | bytes 6148
  82.2 81.4 %all-gather.6.cloned.1.call-start = ((), (), s32[]{:S(2)}) async-start(), calls=%async_computation.6 | async-start | bytes 1179648 | tf_op jit(solution)/shard_map/all_gather | solution.py:210
  83.0 138.6 %all-reduce.12.cloned.1.call-start = ((), (), s32[]{:S(2)}) async-start(), calls=%async_computation.2 | async-start | bytes 2097152 | tf_op jit(solution)/shard_map/psum | solution.py:275
  176.0 47.1 %copy-start.25 = (bf16[512,2,64]{0,2,1:T(8,128)(2,1)}, bf16[512,2,64]{0,2,1:T(8,128)(2,1)S(1)}, u32[]{:S(2)}) copy-start(bf16[512,2,64]{0,2,1:T(8,128)(2,1)S(1)} %convert_element_type.225) | copy-start | bytes 393220
  178.3 86.5 %all-reduce.14.cloned.1.call-start = ((), (), s32[]{:S(2)}) async-start(), calls=%async_computation.3 | async-start | bytes 2097152 | tf_op jit(solution)/shard_map/psum | solution.py:292
  223.0 41.8 %copy-start.7 = (f32[512,512]{0,1:T(8,128)}, f32[512,512]{0,1:T(8,128)S(1)}, u32[]{:S(2)}) copy-start(f32[512,512]{0,1:T(8,128)S(1)} %get-tuple-element.2067) | copy-start | bytes 3145732
  223.0 41.7 %copy-start.52 = (f32[512]{0:T(512)}, f32[512]{0:T(512)S(1)}, u32[]{:S(2)}) copy-start(f32[512]{0:T(512)S(1)} %add_rsqrt_fusion.1) | copy-start | bytes 6148
  223.0 5.4 copy-start.22
  223.1 41.7 %copy-start.56 = (f32[512]{0:T(512)S(1)}, f32[512]{0:T(512)}, u32[]{:S(2)}) copy-start(f32[512]{0:T(512)} %param.45) | copy-start | bytes 6148
  226.7 42.2 %copy-start.20 = (bf16[512,512]{1,0:T(8,128)(2,1)}, bf16[512,512]{1,0:T(8,128)(2,1)S(1)}, u32[]{:S(2)}) copy-start(bf16[512,512]{1,0:T(8,128)(2,1)S(1)} %get-tuple-element.2091) | copy-start | bytes 1572868
  228.1 198.1 %reduce-scatter.2.cloned.1.call-start = ((), (), s32[]{:S(2)}) async-start(), calls=%async_computation.4 | async-start | bytes 4718592 | tf_op jit(solution)/shard_map/reduce_scatter | solution.py:377
  266.9 7.8 copy-start.2
  266.9 7.8 copy-start.3
  310.5 154.5 %all-reduce.16.cloned.1.call-start = ((), (), s32[]{:S(2)}) async-start(), calls=%async_computation.5 | async-start | bytes 2097152 | tf_op jit(solution)/shard_map/psum | solution.py:396
  336.2 93.9 %copy-start.10 = (f32[512,512]{0,1:T(8,128)S(1)}, f32[512,512]{0,1:T(8,128)}, u32[]{:S(2)}) copy-start(f32[512,512]{0,1:T(8,128)} %copy-done.9) | copy-start | bytes 3145732
  336.2 93.9 %copy-start.26 = (bf16[512,2,64]{0,2,1:T(8,128)(2,1)S(1)}, bf16[512,2,64]{0,2,1:T(8,128)(2,1)}, u32[]{:S(2)}) copy-start(bf16[512,2,64]{0,2,1:T(8,128)(2,1)} %copy-done.25) | copy-start | bytes 393220
  336.2 94.9 %copy-start.5 = (f32[512,512]{0,1:T(8,128)S(1)}, f32[512,512]{0,1:T(8,128)}, u32[]{:S(2)}) copy-start(f32[512,512]{0,1:T(8,128)} %copy-done.4) | copy-start | bytes 3145732
  336.2 94.9 %copy-start.51 = (f32[512]{0:T(512)S(1)}, f32[512]{0:T(512)}, u32[]{:S(2)}) copy-start(f32[512]{0:T(512)} %copy-done.50) | copy-start | bytes 6148
  336.2 94.9 %copy-start.55 = (f32[512]{0:T(512)S(1)}, f32[512]{0:T(512)}, u32[]{:S(2)}) copy-start(f32[512]{0:T(512)} %param.42) | copy-start | bytes 6148
  429.8 213.0 %all-reduce.18.cloned.1.call-start = ((), (), s32[]{:S(2)}) async-start(), calls=%async_computation.8 | async-start | bytes 7864320 | tf_op jit(solution)/shard_map/psum | solution.py:424
  431.1 37.3 %copy-start.14 = (f32[512,256]{1,0:T(8,128)S(1)}, f32[512,256]{1,0:T(8,128)}, u32[]{:S(2)}) copy-start(f32[512,256]{1,0:T(8,128)} %copy-done.13) | copy-start | bytes 1572868
  431.1 37.3 %copy-start.49 = (f32[512]{0:T(512)S(1)}, f32[512]{0:T(512)}, u32[]{:S(2)}) copy-start(f32[512]{0:T(512)} %copy-done.48) | copy-start | bytes 6148
  431.1 37.3 %copy-start.59 = (f32[256]{0:T(256)S(1)}, f32[256]{0:T(256)}, u32[]{:S(2)}) copy-start(f32[256]{0:T(256)} %param.40) | copy-start | bytes 3076
  432.5 37.1 %copy-start.30 = (bf16[256,512]{1,0:T(8,128)(2,1)S(1)}, bf16[256,512]{1,0:T(8,128)(2,1)}, u32[]{:S(2)}) copy-start(bf16[256,512]{1,0:T(8,128)(2,1)} %param.41) | copy-start | bytes 786436
  486.3 6.1 copy-start.34
  486.3 6.1 copy-start.65
  492.1 324.3 %all-reduce.20.cloned.1.call-start = ((), (), s32[]{:S(2)}) async-start(), calls=%async_computation.9 | async-start | bytes 18874368 | tf_op jit(solution)/shard_map/psum | solution.py:283
  824.2 23.9 %copy-start.47 = (f32[64,256]{1,0:T(8,128)S(1)}, f32[64,256]{1,0:T(8,128)}, u32[]{:S(2)}) copy-start(f32[64,256]{1,0:T(8,128)} %get-tuple-element.2616) | copy-start | bytes 196612
  824.2 26.4 %copy-start.38 = (f32[128,512]{1,0:T(8,128)S(1)}, f32[128,512]{1,0:T(8,128)}, u32[]{:S(2)}) copy-start(f32[128,512]{1,0:T(8,128)} %get-tuple-element.2621) | copy-start | bytes 786436
  824.3 27.1 %copy-start.28 = (f32[512,512]{1,0:T(8,128)S(1)}, f32[512,512]{1,0:T(8,128)}, u32[]{:S(2)}) copy-start(f32[512,512]{1,0:T(8,128)} %get-tuple-element.2623) | copy-start | bytes 3145732
  825.8 26.5 %copy-start.27 = (f32[512,512]{1,0:T(8,128)S(1)}, f32[512,512]{1,0:T(8,128)}, u32[]{:S(2)}) copy-start(f32[512,512]{1,0:T(8,128)} %get-tuple-element.2624) | copy-start | bytes 3145732
  825.8 27.5 %copy-start.1 = (bf16[512,512]{1,0:T(8,128)(2,1)S(1)}, bf16[512,512]{1,0:T(8,128)(2,1)}, u32[]{:S(2)}) copy-start(bf16[512,512]{1,0:T(8,128)(2,1)} %param.46) | copy-start | bytes 1572868
  (27 other events, 84.0 us)
Sparse Core Ops, SparseCore 0:
  44.7 33.3 all-reduce.9
  82.4 40.1 all-gather.7
  125.2 38.4 all-gather.5
  178.4 43.1 all-reduce.11
  228.3 36.4 all-reduce.13
  310.6 115.5 reduce-scatter.1
  429.9 35.0 all-reduce.15
  492.2 150.5 all-reduce.17
  646.1 170.2 all-reduce.19
where the time goes:
time: 874 us; the launch traced here: 860 us
  waiting for transfers between devices  585 us (67%)
  matrix products  106 us (12%)
  local copies, waits for them, and re-layouts  50.8 us (6%)
  other arithmetic  46.9 us (5%)
  blocking collectives  44.4 us (5%)
  between operations  15.1 us (2%)
  loops' own time  11 us (1%)
    psum x1, waiting for transfers between devices, per_device(): lax.psum(jnp.dot(active_low, ffn_down, preferred_element_type=jnp.float32...  171 us
    psum x1, waiting for transfers between devices, per_device(): lax.psum((grad_char_gain, grad_char_proj, grad_char_out, grad_pool_gain,...  139 us
    reduce_scatter x1, waiting for transfers between devices, per_device(): lax.psum_scatter(lax.fori_loop(0, words_dev * lax.axis_size('seq') // key...  89.8 us
    psum x1, waiting for transfers between devices, per_device(): lax.psum(jnp.dot(mixed_low, attn_out, preferred_element_type=jnp.float32)...  40.6 us
    psum x1, waiting for transfers between devices, per_device(): lax.psum(jnp.einsum('wf,cf->wc', grad_upward, ffn_up, preferred_element_t...  36.1 us
    psum x1, waiting for transfers between devices, per_device(): lax.psum(jnp.dot(pooled_low, char_out, preferred_element_type=jnp.float32...  33 us
    psum x1, waiting for transfers between devices, per_device(): lax.psum(jnp.einsum('swe,sce->wc', grad_mapped, attn_proj, preferred_elem...  32.6 us
    all_gather x1, waiting for transfers between devices, per_device(): lax.all_gather(value_low, 'seq', axis=0, tiled=True)  29.1 us
  transfers between devices with their start and end apart: 9, of which 9 were waited for; matrix products, arithmetic and copies ran while one was open for 6% of the time, Pallas kernels for 0%

commit v1 on v0

v1 whole, which is shorter than its diff:
```python
import functools
from types import SimpleNamespace

import jax
import jax.numpy as jnp
from jax import lax
from jax.experimental import pallas as pl
from jax.experimental.pallas import tpu as pltpu
from jax.sharding import PartitionSpec as P

MESH = pl.DeviceIdType.MESH
BF = jnp.bfloat16
F32 = jnp.float32
EPSILON = 1e-06
NEGATIVE = -1e30

D = 512
C = 256
L = 16
G = 4
Q = 128
W = G * Q
PW = 2 * W
R = Q * L
FS = 512
GROUPS = R // 128
QT = 256
KU = 512
MARKS = 8
SLOTS = 8
FR = 1024
AR = 512

INPUTS = [
    "word_input",
    "char_input",
    "char_count",
    "document_ids",
    "output_grad",
    "char_gain",
    "char_proj",
    "char_out",
    "pool_gain",
    "pool_proj",
    "attn_gain",
    "attn_proj",
    "attn_out",
    "ffn_gain",
    "ffn_up",
    "ffn_down",
]
OUTPUTS = ["o_layer", "o_words", "o_chars", "o_ffn", "o_att", "o_chr", "o_pool", "o_gain"]


def dot(a, b):
    return lax.dot_general(a, b, (((1,), (0,)), ((), ())), preferred_element_type=F32)


def dot_t(a, b):
    return lax.dot_general(a, b, (((1,), (1,)), ((), ())), preferred_element_type=F32)


def dot_l(a, b):
    return lax.dot_general(a, b, (((0,), (0,)), ((), ())), preferred_element_type=F32)


def iota(shape, axis):
    return lax.broadcasted_iota(jnp.int32, shape, axis)


def swap(a):
    return pltpu.roll(a, 64, 1)


def rms_factor(values):
    return lax.rsqrt(jnp.mean(values * values, axis=-1, keepdims=True) + EPSILON)


def rms_back(upstream, values, gain):
    factor = rms_factor(values)
    unit = values * factor
    scaled = upstream * gain
    centre = jnp.mean(scaled * unit, axis=-1, keepdims=True)
    return factor * (scaled - unit * centre), jnp.sum(upstream * unit, axis=0, keepdims=True)


def scratch_list(nz):
    n = 2 * nz
    vm = pltpu.VMEM
    dma = pltpu.SemaphoreType.DMA
    return dict(
        xin=vm((Q, L, C), BF),
        cnt=vm((G, 128), jnp.int32),
        docs=vm((n, G, 128), jnp.int32),
        cpr=vm((3, C, 64), BF),
        win=vm((Q, D), BF),
        ogp=vm((2, W, D), BF),
        cg=vm((1, C), F32),
        pg=vm((1, C), F32),
        ag=vm((1, D), F32),
        fg=vm((1, D), F32),
        cw=vm((G, C, 256), BF),
        cwt=vm((G, C, 256), BF),
        co=vm((G, 128, C), BF),
        pw=vm((C, D), BF),
        aw=vm((G, 3, D, 128), BF),
        ao=vm((G, 128, D), BF),
        fu=vm((G, D, FS), BF),
        fd=vm((G, FS, D), BF),
        low=vm((R, C), BF),
        cntm=vm((128, 128), F32),
        share=vm((GROUPS, 8, 128), F32),
        shc=vm((R, 128), F32),
        msel=vm((GROUPS, 16, 128), BF),
        bias=vm((GROUPS, 128, 128), F32),
        kq=vm((G, R, 256), BF),
        pt=vm((G, GROUPS, 128, 128), BF),
        pooled=vm((G, Q, 128), F32),
        gp=vm((G, Q, 128), F32),
        mean=vm((Q, C), F32),
        summ=vm((Q, C), F32),
        plow=vm((Q, C), BF),
        hid=vm((Q, D), F32),
        alow=vm((Q, D), BF),
        sec=vm((Q, D), F32),
        flow=vm((Q, D), BF),
        lay=vm((Q, D), BF),
        fsum=vm((Q, D), F32),
        act=vm((G, Q, FS), BF),
        lsum=vm((Q, D), F32),
        gsec=vm((Q, D), F32),
        gb=vm((Q, D), BF),
        gw=vm((Q, D), BF),
        gsum=vm((Q, C), F32),
        skv=vm((8, Q, 128), BF),
        sq=vm((8, 64, 128), BF),
        rq=vm((8, 64, 128), BF),
        kv=vm((nz * PW, 128), BF),
        marks=vm((min(n, MARKS) * KU, 128), BF),
        qd=vm((PW, 256), BF),
        m=vm((PW, 128), F32),
        l=vm((PW, 128), F32),
        acc=vm((PW, 128), F32),
        ob=vm((PW, 128), BF),
        lser=vm((PW // QT, 8, QT), F32),
        dlr=vm((PW // QT, 8, QT), F32),
        smx=vm((8, 64, 128), BF),
        rmx=vm((8, 64, 128), BF),
        sgm=vm((8, 64, 128), BF),
        rgm=vm((8, 64, 128), BF),
        gz=vm((PW, 128), BF),
        xg=vm((PW, 128), BF),
        acck=vm((KU, 128), F32),
        accv=vm((KU, 128), F32),
        dq=vm((PW, 128), F32),
        dkv=vm((PW, 128), F32),
        sdk=vm((min(n, SLOTS), KU, 128), BF),
        rdk=vm((nz, 2, KU, 128), BF),
        dqb=vm((PW, 128), BF),
        sdkv=vm((8, Q, 128), BF),
        rdkv=vm((8, Q, 128), BF),
        sdq=vm((8, 64, 128), BF),
        rdq=vm((8, 64, 128), BF),
        alp=vm((PW, D), BF),
        flp=vm((PW, D), BF),
        gbp=vm((PW, D), BF),
        sag=vm((8, Q, 512), BF),
        rag=vm((PW, 512), BF),
        fw=vm((FR, 256), BF),
        frs=vm((nz, FR // nz, 256), BF),
        ffin=vm((FR // nz, 256), BF),
        aw_g=vm((AR, 256), BF),
        ars=vm((nz, AR // nz, 256), BF),
        afin=vm((AR // nz, 256), BF),
        scw=vm((G, C, 256), BF),
        rcw=vm((8, 128, 256), BF),
        zcw=vm((nz, 128, 256), BF),
        cfin=vm((128, 256), BF),
        spw=vm((C, D), BF),
        rpw=vm((8, 32, D), BF),
        zpw=vm((nz, 32, D), BF),
        pfin=vm((32, D), BF),
        gn=vm((8, D), F32),
        rgn=vm((8, 8, D), F32),
        zgn=vm((nz, 8, D), F32),
        gnf=vm((8, D), F32),
        lsem=dma((24,)),
        wg_s=dma((6, 3)),
        wg_r=dma((6, 3)),
        kv_s=dma((8,)),
        kv_r=dma((8,)),
        q_s=dma((8,)),
        q_r=dma((8,)),
        mx_s=dma((8,)),
        mx_r=dma((8,)),
        gm_s=dma((8,)),
        gm_r=dma((8,)),
        dkv_s=dma((8,)),
        dkv_r=dma((8,)),
        dq_s=dma((8,)),
        dq_r=dma((8,)),
        al_s=dma((8,)),
        al_r=dma((8,)),
        fl_s=dma((8,)),
        fl_r=dma((8,)),
        gb_s=dma((8,)),
        gb_r=dma((8,)),
        ac_s=dma((8,)),
        ac_r=dma((8,)),
        cw_s=dma((8,)),
        cw_r=dma((8,)),
        pw_s=dma((8,)),
        pw_r=dma((8,)),
        pa_s=dma((8,)),
        pa_r=dma((8,)),
        gn_s=dma((8,)),
        gn_r=dma((8,)),
        kz_s=dma((n,)),
        kz_r=dma((n,)),
        dz_s=dma((nz,)),
        dz_r=dma((nz,)),
        x_s=dma((5,)),
        x_r=dma((5,)),
        dk_s=dma((n,)),
        dk_r=dma((nz, 2)),
        fr_s=dma((nz,)),
        fr_r=dma((nz,)),
        fa_s=dma((nz,)),
        fa_r=dma((nz,)),
        ar_s=dma((nz,)),
        ar_r=dma((nz,)),
        aa_s=dma((nz,)),
        aa_r=dma((nz,)),
        cz_s=dma((nz,)),
        cz_r=dma((nz,)),
        pz_s=dma((nz,)),
        pz_r=dma((nz,)),
        gz_s=dma((nz,)),
        gz_r=dma((nz,)),
        ly_s=dma((4,)),
        ly_r=dma((4,)),
        gw_s=dma((4,)),
        gw_r=dma((4,)),
    )


def rows(index, size):
    return pl.ds(pl.multiple_of(index * size, size), size)


def layer_kernel(nz, names, *refs):
    r = SimpleNamespace(**dict(zip(names, refs)))
    s = lax.axis_index("seq")
    h = lax.axis_index("head")
    x, z = lax.rem(s, 2), lax.div(s, 2)
    y, c = lax.div(h, 2), lax.rem(h, 2)
    p = 4 * x + h
    sends = []

    def peer(mask):
        px = 1 - x if mask & 4 else x
        py = 1 - y if mask & 2 else y
        pc = 1 - c if mask & 1 else c
        ph = 2 * py + pc
        return (2 * z + px, ph), 4 * px + ph

    def plane(t):
        pz = lax.rem(z + t, nz)
        return (2 * pz + x, h), pz

    def remote(src, dst, ssem, rsem, device):
        return pltpu.make_async_remote_copy(
            src_ref=src, dst_ref=dst, send_sem=ssem, recv_sem=rsem,
            device_id=device, device_id_type=MESH,
        )

    def send(src, dst, ssem, rsem, device):
        copy = remote(src, dst, ssem, rsem, device)
        copy.start()
        sends.append(copy)

    def arrive(dst, ssem, rsem):
        remote(dst, dst, ssem, rsem, peer(1)[0]).wait_recv()

    def load(src, dst, k):
        copy = pltpu.make_async_copy(src, dst, r.lsem.at[k])
        copy.start()
        return copy

    low_half = iota((1, 128), 1) < 64

    def pick(a, b):
        shape = a.shape
        return jnp.where(iota(shape, 1) < 64, a, b)

    def pack(a):
        return pick(a[:64], swap(a[64:]))

    def pack_high(a):
        return pick(swap(a[:64]), a[64:])

    barrier = pltpu.get_barrier_semaphore()
    for mask in range(1, 8):
        pl.semaphore_signal(barrier, inc=1, device_id=peer(mask)[0], device_id_type=MESH)
    for t in range(1, nz):
        pl.semaphore_signal(barrier, inc=1, device_id=plane(t)[0], device_id_type=MESH)

    ld_x = load(r.char_input.at[rows(h, Q)], r.xin, 0)
    ld_cg = load(r.char_gain, r.cg, 1)
    ld_cnt = load(r.char_count, r.cnt, 2)
    ld_cp = load(r.char_proj, r.cpr, 3)
    ld_doc = load(r.document_ids, r.docs.at[s], 4)
    ld_co = load(r.char_out, r.co.at[h, pl.ds(64, 64)], 5)
    ld_pw = load(r.pool_proj, r.pw, 6)
    ld_word = load(r.word_input.at[rows(h, Q)], r.win, 7)
    ld_pg = load(r.pool_gain, r.pg, 8)
    ld_ag = load(r.attn_gain, r.ag, 9)
    ld_fg = load(r.ffn_gain, r.fg, 10)
    ld_aw = load(r.attn_proj, r.aw.at[h], 11)
    ld_ao = load(r.attn_out, r.ao.at[h], 12)
    ld_og = load(r.output_grad, r.ogp.at[x], 13)
    ld_fu = load(r.ffn_up, r.fu.at[h], 14)
    ld_fd = load(r.ffn_down, r.fd.at[h], 15)

    r.co[:, 0:64, :] = jnp.zeros((G, 64, C), BF)

    ld_cp.wait()
    place = (iota((64, 128), 0) == iota((64, 128), 1)).astype(F32).astype(BF)
    place_high = (iota((64, 128), 0) + 64 == iota((64, 128), 1)).astype(F32).astype(BF)
    wq, wk, wv = r.cpr[0], r.cpr[1], r.cpr[2]
    r.cw[h, :, 0:128] = (dot(wk, place) + dot(wq, place_high)).astype(BF)
    r.cw[h, :, 128:256] = (dot(wq, place) + dot(wv, place_high)).astype(BF)

    ld_x.wait()
    ld_cg.wait()

    def char_norm(i, carry):
        values = r.xin[pl.ds(i * 8, 8)].astype(F32).reshape(128, C)
        r.low[rows(i, 128), :] = (values * rms_factor(values) * r.cg[...]).astype(BF)
        return carry

    lax.fori_loop(0, GROUPS, char_norm, 0, unroll=2)

    ld_cnt.wait()
    count_row = jnp.broadcast_to(r.cnt[pl.ds(h, 1), :].astype(F32), (128, 128))
    r.cntm[...] = count_row.T

    def char_masks(g, carry):
        eight = r.cntm[rows(g, 8), :]
        lane8 = iota((8, 128), 1)
        of_lane = jnp.sum(
            jnp.where(iota((8, 128), 0) == lax.div(lane8, L), eight, 0.0), axis=0, keepdims=True
        )
        lane16 = iota((16, 128), 1)
        count16 = jnp.broadcast_to(of_lane, (16, 128))
        letter16 = lax.rem(lane16, L).astype(F32)
        r.share[g] = jnp.where(letter16 < count16, 1.0 / count16, 0.0)[:8]
        r.msel[g] = jnp.where(
            (iota((16, 128), 0) == lax.div(lane16, L)) & (letter16 < count16), 1.0, 0.0
        ).astype(BF)
        row, lane = iota((128, 128), 0), iota((128, 128), 1)
        spread = jnp.where(lane == g * 8 + lax.div(row, L), 1.0, 0.0).astype(BF)
        count = dot(spread, r.cntm[...].astype(BF))
        valid = lax.rem(row, L).astype(F32) < count
        r.bias[g] = jnp.where(valid & (lax.div(row, L) == lax.div(lane, L)), 0.0, NEGATIVE)
        r.shc[rows(g, 128), :] = jnp.where(valid, 1.0 / count, 0.0)
        return carry

    lax.fori_loop(0, GROUPS, char_masks, 0)

    pl.semaphore_wait(barrier, 7 + nz - 1)

    def gather_start(k, slots):
        mine = slots(h)
        send(mine, mine, r.wg_s.at[k, 0], r.wg_r.at[k, 0], peer(1)[0])
        send(mine, mine, r.wg_s.at[k, 1], r.wg_r.at[k, 1], peer(2)[0])

    def gather_forward(k, slots):
        far = slots(2 * (1 - y) + c)
        arrive(far, r.wg_s.at[k, 1], r.wg_r.at[k, 1])
        send(far, far, r.wg_s.at[k, 2], r.wg_r.at[k, 2], peer(1)[0])

    def gather_near(k, slots):
        arrive(slots(2 * y + 1 - c), r.wg_s.at[k, 0], r.wg_r.at[k, 0])

    def gather_last(k, slots):
        arrive(slots(2 * (1 - y) + 1 - c), r.wg_s.at[k, 2], r.wg_r.at[k, 2])

    order = [h, 2 * y + 1 - c, 2 * (1 - y) + c, 2 * (1 - y) + 1 - c]
    cw_at = lambda i: r.cw.at[i]
    co_at = lambda i: r.co.at[i, pl.ds(64, 64)]
    aw_at = lambda i: r.aw.at[i]
    ao_at = lambda i: r.ao.at[i]
    fu_at = lambda i: r.fu.at[i]
    fd_at = lambda i: r.fd.at[i]

    gather_start(0, cw_at)
    ld_co.wait()
    gather_start(1, co_at)
    ld_doc.wait()
    send(r.docs.at[s], r.docs.at[s], r.x_s.at[0], r.x_r.at[0], peer(4)[0])
    ld_aw.wait()
    gather_start(2, aw_at)

    lane_scale = jnp.where((iota((1, 256), 1) < 64) | (iota((1, 256), 1) >= 192), 1.0, 0.125)
    keep_low = jnp.where(low_half, 1.0, 0.0)
    keep_high = 1.0 - keep_low

    def char_head(hh):
        def project(i, carry):
            got = dot(r.low[rows(i, 512), :], r.cw[hh]) * lane_scale
            r.kq[hh, rows(i, 512), :] = got.astype(BF)
            return carry

        lax.fori_loop(0, R // 512, project, 0)

        def attend(g, carry):
            kq = r.kq[hh, rows(g, 128), 0:128]
            qv = r.kq[hh, rows(g, 128), 128:256]
            query = (qv.astype(F32) * keep_low).astype(BF)
            scores = dot_t(kq, query) + r.bias[g]
            raised = jnp.exp(scores - jnp.max(scores, axis=0, keepdims=True))
            weights = (raised * (1.0 / jnp.sum(raised, axis=0, keepdims=True))).astype(BF)
            r.pt[hh, g] = weights
            taken = dot_t(r.msel[g], weights).astype(BF)
            got = dot(taken, qv)[:8] * (1.0 / r.cntm[rows(g, 8), :])
            r.pooled[hh, rows(g, 8), :] = got * keep_high
            return carry

        lax.fori_loop(0, GROUPS, attend, 0, unroll=4)

    char_head(order[0])
    gather_near(0, cw_at)
    char_head(order[1])
    gather_forward(0, cw_at)
    gather_forward(1, co_at)
    gather_forward(2, aw_at)
    char_head(order[2])
    gather_last(0, cw_at)
    char_head(order[3])

    def char_mean(g, carry):
        block = r.xin[pl.ds(g * 8, 8)].reshape(128, C)
        r.mean[rows(g, 8), :] = dot(r.msel[g], block)[:8] * (1.0 / r.cntm[rows(g, 8), 0:1])
        return carry

    lax.fori_loop(0, GROUPS, char_mean, 0, unroll=4)
    gather_near(1, co_at)
    gather_last(1, co_at)
    summary = r.mean[...]
    for hh in range(G):
        summary = summary + dot(r.pooled[hh].astype(BF), r.co[hh])
    r.summ[...] = summary
    ld_pg.wait()
    ld_pw.wait()
    ld_word.wait()
    ld_ag.wait()
    r.plow[...] = (summary * rms_factor(summary) * r.pg[...]).astype(BF)
    hidden = r.win[...].astype(F32) + dot(r.plow[...], r.pw[...])
    r.hid[...] = hidden
    r.alow[...] = (hidden * rms_factor(hidden) * r.ag[...]).astype(BF)

    gather_near(2, aw_at)
    gather_last(2, aw_at)
    kv_mine = lambda i: r.kv.at[rows(z * 8 + i, Q)]
    for t in range(G):
        hh = order[t]
        query = dot(r.alow[...], r.aw[hh, 0]) * 0.125
        key = dot(r.alow[...], r.aw[hh, 1])
        value = dot(r.alow[...], r.aw[hh, 2])
        r.skv[hh] = pick(key, swap(value)).astype(BF)
        r.skv[4 + hh] = pick(swap(key), value).astype(BF)
        r.sq[hh] = pack(query).astype(BF)
        r.sq[4 + hh] = pack_high(query).astype(BF)
        for mask in ((4,) if t == 0 else (t, t + 4)):
            device, to = peer(mask)
            send(r.skv.at[to], kv_mine(p), r.kv_s.at[mask], r.kv_r.at[mask], device)
            send(r.sq.at[to], r.rq.at[p], r.q_s.at[mask], r.q_r.at[mask], device)
    r.kv[rows(z * 8 + p, Q), :] = r.skv[p]
    r.rq[p] = r.sq[p]

    arrive(r.docs.at[2 * z + 1 - x], r.x_s.at[0], r.x_r.at[0])
    docs_mine = r.docs.at[pl.ds(2 * z, 2)]

    def docs_copy(t, source):
        return remote(
            r.docs.at[pl.ds(2 * source, 2)], r.docs.at[pl.ds(2 * source, 2)],
            r.dz_s.at[t], r.dz_r.at[source], (2 * lax.rem(z + t, nz) + x, h),
        )

    for t in range(1, nz):
        @pl.when(z + t < nz)
        def _():
            docs_copy(t, z).start()

    def key_marks(chunk, carry):
        row = r.docs[lax.div(chunk, 4), pl.ds(lax.rem(chunk, 4), 1), :]
        sub = iota((128, 128), 0)
        marks = jnp.where((sub < 3) & (jnp.broadcast_to(row, (128, 128)) != sub), 1.0, 0.0)
        slot = lax.rem(chunk, 4 * min(2 * nz, MARKS))
        r.marks[rows(slot, 128), :] = marks.T.astype(BF)
        return carry

    def query_marks(chunk, carry):
        row = r.docs[lax.div(z * 8 + chunk, 4), pl.ds(lax.rem(chunk, 4), 1), :]
        sub = iota((128, 128), 0)
        marks = jnp.where((sub < 3) & (jnp.broadcast_to(row, (128, 128)) == sub), NEGATIVE, 0.0)
        r.qd[rows(chunk, 128), 128:256] = marks.T.astype(BF)
        return carry

    lax.fori_loop(z * 8, z * 8 + 8, key_marks, 0)
    lax.fori_loop(0, 8, query_marks, 0)
    r.m[...] = jnp.full((PW, 128), NEGATIVE, F32)
    r.l[...] = jnp.zeros((PW, 128), F32)
    r.acc[...] = jnp.zeros((PW, 128), F32)

    for mask in range(1, 8):
        arrive(kv_mine(peer(mask)[1]), r.kv_s.at[mask], r.kv_r.at[mask])

    def unit_copy(u):
        block = r.kv.at[rows(u, KU)]
        return remote(
            block, block, r.kz_s.at[u], r.kz_r.at[u], (2 * lax.rem(z + 1, nz) + x, h)
        )

    @pl.when(z + 1 < nz)
    def _():
        unit_copy(2 * z).start()
        unit_copy(2 * z + 1).start()

    for mask in range(1, 8):
        arrive(r.rq.at[peer(mask)[1]], r.q_s.at[mask], r.q_r.at[mask])

    def unpack_queries(i, carry):
        got = r.rq[i].astype(F32)
        r.qd[rows(2 * i, 64), 0:128] = (got * keep_low).astype(BF)
        r.qd[rows(2 * i + 1, 64), 0:128] = (swap(got) * keep_low).astype(BF)
        return carry

    lax.fori_loop(0, 8, unpack_queries, 0)

    ld_ao.wait()
    gather_start(3, ao_at)
    ld_fu.wait()
    gather_start(4, fu_at)
    ld_fd.wait()
    gather_start(5, fd_at)
    ld_og.wait()
    send(r.ogp.at[x], r.ogp.at[x], r.x_s.at[1], r.x_r.at[1], peer(4)[0])
    for mask in range(1, 8):
        send(r.alow, r.alp.at[rows(p, Q)], r.al_s.at[mask], r.al_r.at[mask], peer(mask)[0])
    r.alp[rows(p, Q), :] = r.alow[...]

    def marked(kv, u):
        marks = r.marks[rows(lax.rem(u, min(2 * nz, MARKS)), KU), :]
        return jnp.concatenate([kv, marks], axis=1)

    def mark_again(u):
        if 2 * nz > MARKS:
            lax.fori_loop(4 * u, 4 * u + 4, key_marks, 0)

    def forward_tile(qt, u, causal):
        at = rows(qt, QT)
        kv = r.kv[rows(u, KU), :]
        scores = dot_t(r.qd[at, :], marked(kv, u))
        if causal:
            gap = (qt * QT - (u - 2 * z) * KU) + iota((QT, KU), 0) - iota((QT, KU), 1)
            scores = jnp.where(gap >= 0, scores, NEGATIVE)
        old = r.m[at, :]
        new = jnp.maximum(old, jnp.max(scores, axis=1, keepdims=True))
        raised = jnp.exp(scores - new[:, 0:1])
        fade = jnp.exp(old - new)
        r.m[at, :] = new
        r.l[at, :] = r.l[at, :] * fade + jnp.sum(raised, axis=1, keepdims=True)
        r.acc[at, :] = r.acc[at, :] * fade + dot(raised.astype(BF), kv)

    def forward_first(qt, carry):
        forward_tile(qt, 2 * z, True)
        return carry

    def forward_second(qt, carry):
        forward_tile(qt, 2 * z + 1, True)
        return carry

    lax.fori_loop(0, PW // QT, forward_first, 0)
    lax.fori_loop(KU // QT, PW // QT, forward_second, 0)

    def wait_docs(source, carry):
        docs_copy(1, source).wait_recv()
        return carry

    lax.fori_loop(0, z, wait_docs, 0)
    if 2 * nz <= MARKS:
        lax.fori_loop(0, z * 8, key_marks, 0)

    def forward_unit(i, carry):
        u = 2 * z - 1 - i
        unit_copy(u).wait_recv()
        mark_again(u)

        @pl.when(z + 1 < nz)
        def _():
            unit_copy(u).start()

        def step(qt, inner):
            forward_tile(qt, u, False)
            return inner

        return lax.fori_loop(0, PW // QT, step, carry)

    lax.fori_loop(0, 2 * z, forward_unit, 0)

    def finish_rows(qt, carry):
        for half in range(2):
            i = 2 * qt + half
            at = rows(i, 128)
            total = r.l[at, :]
            out = r.acc[at, :] * (1.0 / total) * keep_high
            r.acc[at, :] = out
            r.ob[at, :] = out.astype(BF)
            r.smx[i] = pack_high(out).astype(BF)
            lse = (r.m[at, :] + jnp.log(total)).T
            r.lser[qt, :, half * 128 : half * 128 + 128] = lse[:8]
        return carry

    lax.fori_loop(0, PW // QT, finish_rows, 0)
    for mask in range(1, 8):
        device, to = peer(mask)
        send(r.smx.at[to], r.rmx.at[p], r.mx_s.at[mask], r.mx_r.at[mask], device)
    r.rmx[p] = r.smx[p]
    gather_forward(3, ao_at)
    gather_forward(4, fu_at)
    gather_forward(5, fd_at)
    gather_near(3, ao_at)
    gather_last(3, ao_at)
    ld_fg.wait()
    for mask in range(1, 8):
        arrive(r.rmx.at[peer(mask)[1]], r.mx_s.at[mask], r.mx_r.at[mask])

    def two_heads(a, b):
        a, b = a.astype(F32), b.astype(F32)
        return jnp.concatenate([pick(a, swap(b)), pick(swap(a), b)], axis=0).astype(BF)

    second = r.hid[...]
    for hh in range(G):
        second = second + dot(two_heads(r.rmx[hh], r.rmx[4 + hh]), r.ao[hh])
    r.sec[...] = second
    r.flow[...] = (second * rms_factor(second) * r.fg[...]).astype(BF)

    grad_rows = r.ogp[x, rows(h, Q), :]
    r.fsum[...] = jnp.zeros((Q, D), F32)
    for t in range(G):
        hh = order[t]
        if t == 1:
            gather_near(4, fu_at)
            gather_near(5, fd_at)
        if t == 3:
            gather_last(4, fu_at)
            gather_last(5, fd_at)
        upward = dot(r.flow[...], r.fu[hh])
        square = upward * upward
        inner = 0.7978845608028654 * upward * (1.0 + 0.044715 * square)
        bent = jnp.tanh(inner)
        half_up = 0.5 * (1.0 + bent)
        active = (upward * half_up).astype(BF)
        slope = half_up + 0.5 * upward * (1.0 - bent * bent) * (
            0.7978845608028654 * (1.0 + 0.134145 * square)
        )
        r.act[hh] = active
        grad_up = (dot_t(grad_rows, r.fd[hh]) * slope).astype(BF)
        r.fsum[...] += dot_t(grad_up, r.fu[hh])
        r.sag[hh, :, 0:256] = active[:, 0:256]
        r.sag[hh, :, 256:512] = grad_up[:, 0:256]
        r.sag[4 + hh, :, 0:256] = active[:, 256:512]
        r.sag[4 + hh, :, 256:512] = grad_up[:, 256:512]
    back, gain_ffn = rms_back(r.fsum[...], r.sec[...], r.fg[...])
    grad_second = grad_rows.astype(F32) + back
    r.gsec[...] = grad_second
    r.gb[...] = grad_second.astype(BF)
    r.gn[0:1, :] = gain_ffn

    for t in range(G):
        hh = order[t]
        grad = dot_t(r.gb[...], r.ao[hh])
        r.sgm[hh] = pack(grad).astype(BF)
        r.sgm[4 + hh] = pack_high(grad).astype(BF)
        for mask in ((4,) if t == 0 else (t, t + 4)):
            device, to = peer(mask)
            send(r.sgm.at[to], r.rgm.at[p], r.gm_s.at[mask], r.gm_r.at[mask], device)
    r.rgm[p] = r.sgm[p]
    r.dq[...] = jnp.zeros((PW, 128), F32)
    r.lsum[...] = r.sec[...]

    def layer_part(hh, carry):
        r.lsum[...] += dot(r.act[hh], r.fd[hh])
        return carry

    lax.fori_loop(0, G, layer_part, 0)
    r.lay[...] = r.lsum[...].astype(BF)
    for mask in range(1, 8):
        arrive(r.rgm.at[peer(mask)[1]], r.gm_s.at[mask], r.gm_r.at[mask])

    def unpack_grads(qt, carry):
        for half in range(2):
            i = 2 * qt + half
            at = rows(i, 128)
            got = r.rgm[i].astype(F32)
            grad = jnp.concatenate([swap(got), got], axis=0) * keep_high
            r.gz[at, :] = grad.astype(BF)
            r.xg[at, :] = pick(r.qd[at, 0:128].astype(F32), grad).astype(BF)
            delta = jnp.sum(grad * r.acc[at, :], axis=1, keepdims=True)
            r.dlr[qt, :, half * 128 : half * 128 + 128] = jnp.broadcast_to(delta, (128, 128)).T[:8]
        return carry

    lax.fori_loop(0, PW // QT, unpack_grads, 0)

    for mask in range(1, 8):
        device, to = peer(mask)
        send(r.sag.at[to], r.rag.at[rows(p, Q)], r.ac_s.at[mask], r.ac_r.at[mask], device)
        send(r.flow, r.flp.at[rows(p, Q)], r.fl_s.at[mask], r.fl_r.at[mask], device)
        send(r.gb, r.gbp.at[rows(p, Q)], r.gb_s.at[mask], r.gb_r.at[mask], device)
    r.rag[rows(p, Q), :] = r.sag[p]
    r.flp[rows(p, Q), :] = r.flow[...]
    r.gbp[rows(p, Q), :] = r.gb[...]
    for mask in range(1, 4):
        mine = r.o_layer.at[rows(h, Q)]
        send(r.lay, mine, r.ly_s.at[mask], r.ly_r.at[mask], peer(mask)[0])
    st_lay = load(r.lay, r.o_layer.at[rows(h, Q)], 16)

    def backward_tile(qt, u, causal):
        at = rows(qt, QT)
        kv = r.kv[rows(u, KU), :]
        scores = dot_t(marked(kv, u), r.qd[at, :])
        weights = jnp.exp(scores - r.lser[qt, 0:1, :])
        if causal:
            gap = (qt * QT - (u - 2 * z) * KU) + iota((KU, QT), 1) - iota((KU, QT), 0)
            weights = jnp.where(gap >= 0, weights, 0.0)
        dweights = dot_t(kv, r.gz[at, :])
        dscores = (weights * (dweights - r.dlr[qt, 0:1, :])).astype(BF)
        other = r.xg[at, :]
        r.acck[...] += dot(dscores, other)
        r.accv[...] += dot(weights.astype(BF), other)
        r.dq[at, :] += dot_l(dscores, kv)

    def clear_unit():
        r.acck[...] = jnp.zeros((KU, 128), F32)
        r.accv[...] = jnp.zeros((KU, 128), F32)

    def grad_copy(u):
        pz = lax.div(u, 2)
        return remote(
            r.sdk.at[lax.rem(u, min(2 * nz, SLOTS))], r.rdk.at[z, lax.rem(u, 2)], r.dk_s.at[u], r.dk_r.at[z, lax.rem(u, 2)],
            (2 * pz + x, h),
        )

    def backward_unit(u, carry):
        clear_unit()
        mark_again(u)
        if 2 * nz > SLOTS:
            @pl.when(u >= SLOTS)
            def _():
                grad_copy(u - SLOTS).wait_send()

        def step(qt, inner):
            backward_tile(qt, u, False)
            return inner

        lax.fori_loop(0, PW // QT, step, 0)
        r.sdk[lax.rem(u, min(2 * nz, SLOTS))] = pick(r.acck[...], r.accv[...]).astype(BF)
        grad_copy(u).start()
        return carry

    lax.fori_loop(0, 2 * z, backward_unit, 0)
    for own in range(2):
        clear_unit()
        mark_again(2 * z + own)

        def own_step(qt, carry):
            backward_tile(qt, 2 * z + own, True)
            return carry

        lax.fori_loop(own * (KU // QT), PW // QT, own_step, 0)
        r.dkv[own * KU : own * KU + KU, :] = pick(r.acck[...], r.accv[...])

    def all_arrive(dst, ssem, rsem):
        for mask in range(1, 8):
            arrive(dst.at[rows(peer(mask)[1], Q)], ssem.at[mask], rsem.at[mask])

    all_arrive(r.rag, r.ac_s, r.ac_r)
    all_arrive(r.flp, r.fl_s, r.fl_r)
    arrive(r.ogp.at[1 - x], r.x_s.at[1], r.x_r.at[1])
    for i in range(2):
        r.fw[i * 256 : i * 256 + 256, :] = dot_l(
            r.flp[:, i * 256 : i * 256 + 256], r.rag[:, 256:512]
        ).astype(BF)
        r.fw[512 + i * 256 : 768 + i * 256, :] = (
            dot_l(r.rag[0:W, 0:256], r.ogp[0, :, i * 256 : i * 256 + 256])
            + dot_l(r.rag[W:PW, 0:256], r.ogp[1, :, i * 256 : i * 256 + 256])
        ).astype(BF)

    def spread_start(src, size, slots, ssem, rsem):
        for t in range(1, nz):
            device, pz = plane(t)
            send(src.at[rows(pz, size)], slots.at[z], ssem.at[t], rsem.at[z], device)

    def spread_sum(src, size, slots, ssem, rsem):
        slots[z] = src[rows(z, size), :]
        for t in range(1, nz):
            pz = plane(t)[1]
            arrive(slots.at[pz], ssem.at[t], rsem.at[pz])
        total = slots[0].astype(F32)
        for i in range(1, nz):
            total = total + slots[i].astype(F32)
        return total.astype(BF)

    def final_start(src, out, size, ssem, rsem, lk):
        mine = out.at[x, rows(z, size)]
        for t in range(1, nz):
            send(src, mine, ssem.at[t], rsem.at[z], plane(t)[0])
        return load(src, mine, lk)

    def final_cross(out, size, ssem, rsem, copy, k):
        copy.wait()
        for t in range(1, nz):
            pz = plane(t)[1]
            arrive(out.at[x, rows(pz, size)], ssem.at[t], rsem.at[pz])
        send(out.at[x], out.at[x], r.x_s.at[k], r.x_r.at[k], peer(4)[0])

    spread_start(r.fw, FR // nz, r.frs, r.fr_s, r.fr_r)

    def add_grads(pz, carry):
        for own in range(2):
            part = r.rdk.at[pz, own]
            remote(part, part, r.dk_s.at[own], r.dk_r.at[pz, own], peer(1)[0]).wait_recv()
            r.dkv[own * KU : own * KU + KU, :] += r.rdk[pz, own].astype(F32)
        return carry

    lax.fori_loop(z + 1, nz, add_grads, 0)

    def back_rows(i, carry):
        at = rows(i, 128)
        r.sdkv[i] = r.dkv[at, :].astype(BF)
        grad = r.dq[at, :] * 0.125
        r.sdq[i] = pack(grad).astype(BF)
        r.dqb[at, :] = (grad * keep_low).astype(BF)
        return carry

    lax.fori_loop(0, 8, back_rows, 0)
    for mask in range(1, 8):
        device, to = peer(mask)
        send(r.sdkv.at[to], r.rdkv.at[p], r.dkv_s.at[mask], r.dkv_r.at[mask], device)
        send(r.sdq.at[to], r.rdq.at[p], r.dq_s.at[mask], r.dq_r.at[mask], device)
    r.rdkv[p] = r.sdkv[p]
    r.rdq[p] = r.sdq[p]

    all_arrive(r.alp, r.al_s, r.al_r)
    all_arrive(r.gbp, r.gb_s, r.gb_r)
    for i in range(2):
        cols = slice(i * 256, i * 256 + 256)
        r.aw_g[cols, 0:128] = (
            dot_l(r.alp[:, cols], r.dqb[...]) + dot_l(r.gbp[:, cols], r.ob[...])
        ).astype(BF)
        r.aw_g[cols, 128:256] = dot_l(r.alp[:, cols], r.sdkv[...].reshape(PW, 128)).astype(BF)
    spread_start(r.aw_g, AR // nz, r.ars, r.ar_s, r.ar_r)

    for mask in range(1, 8):
        arrive(r.rdkv.at[peer(mask)[1]], r.dkv_s.at[mask], r.dkv_r.at[mask])
        arrive(r.rdq.at[peer(mask)[1]], r.dq_s.at[mask], r.dq_r.at[mask])

    attn_sum = jnp.zeros((Q, D), F32)
    for hh in range(G):
        first, other = r.rdkv[hh].astype(F32), r.rdkv[4 + hh].astype(F32)
        attn_sum = attn_sum + dot_t(two_heads(r.rdq[hh], r.rdq[4 + hh]), r.aw[hh, 0])
        attn_sum = attn_sum + dot_t(pick(first, swap(other)).astype(BF), r.aw[hh, 1])
        attn_sum = attn_sum + dot_t(pick(swap(first), other).astype(BF), r.aw[hh, 2])
    back, gain_attn = rms_back(attn_sum, r.hid[...], r.ag[...])
    r.gw[...] = (r.gsec[...] + back).astype(BF)
    r.gn[1:2, :] = gain_attn
    for mask in range(1, 4):
        mine = r.o_words.at[rows(h, Q)]
        send(r.gw, mine, r.gw_s.at[mask], r.gw_r.at[mask], peer(mask)[0])
    st_gw = load(r.gw, r.o_words.at[rows(h, Q)], 17)
    grad_summary, gain_pool = rms_back(dot_t(r.gw[...], r.pw[...]), r.summ[...], r.pg[...])
    r.gsum[...] = grad_summary
    gs_low = grad_summary.astype(BF)
    r.gn[2:3, 0:256] = gain_pool
    r.spw[...] = dot_l(r.plow[...], r.gw[...]).astype(BF)
    for mask in range(1, 8):
        device, to = peer(mask)
        send(r.spw.at[rows(to, 32)], r.rpw.at[p], r.pw_s.at[mask], r.pw_r.at[mask], device)
    r.rpw[p] = r.spw[rows(p, 32), :]

    r.ffin[...] = spread_sum(r.fw, FR // nz, r.frs, r.fr_s, r.fr_r)
    st_ffn = final_start(r.ffin, r.o_ffn, FR // nz, r.fa_s, r.fa_r, 18)

    def char_head_back(hh):
        r.gp[hh] = dot_t(gs_low, r.co[hh])
        w = r.cw[hh].astype(F32)
        r.cwt[hh, :, 0:128] = swap(w[:, 0:128]).astype(BF)
        r.cwt[hh, :, 128:256] = (w[:, 128:256] * keep_high).astype(BF)

        def attend(g, carry):
            at = rows(g, 128)
            kq = r.kq[hh, at, 0:128]
            value = r.kq[hh, at, 128:256].astype(F32)
            grad8 = r.gp[hh, rows(g, 8), :]
            grad = jnp.broadcast_to(grad8[:, None, :], (8, L, 128)).reshape(128, 128)
            weights = r.pt[hh, g].astype(F32)
            share = r.share[g, 0:1, :]
            gain = jnp.sum(value * grad, axis=1, keepdims=True)
            lifted = weights * gain
            centre = jnp.sum(lifted, axis=0, keepdims=True)
            dscores = ((lifted - weights * centre) * share).astype(BF)
            taken = jnp.sum(weights * share, axis=1, keepdims=True)
            grads = pick(dot_l(dscores, kq) * 0.125, dot(dscores, kq))
            r.kq[hh, at, 0:128] = grads.astype(BF)
            r.kq[hh, at, 128:256] = (taken * grad).astype(BF)
            return carry

        lax.fori_loop(0, GROUPS, attend, 0, unroll=4)
        term = dot_l(r.low[...], r.kq[hh])
        pooled = swap(r.pooled[hh]).astype(BF)
        r.scw[hh, :, 0:128] = term[:, 0:128].astype(BF)
        r.scw[hh, :, 128:256] = (term[:, 128:256] + dot_l(gs_low, pooled)).astype(BF)

    for t in (3, 2, 1, 0):
        hh = order[t]
        char_head_back(hh)
        for mask in ((4,) if t == 0 else (t, t + 4)):
            device, to = peer(mask)
            px = 1 - x if mask & 4 else x
            send(
                r.scw.at[hh, rows(px, 128)], r.rcw.at[p], r.cw_s.at[mask], r.cw_r.at[mask], device
            )
    r.rcw[p] = r.scw[h, rows(x, 128), :]

    r.afin[...] = spread_sum(r.aw_g, AR // nz, r.ars, r.ar_s, r.ar_r)
    st_att = final_start(r.afin, r.o_att, AR // nz, r.aa_s, r.aa_r, 19)

    def plane_sum(slots, ssem, rsem):
        for mask in range(1, 8):
            arrive(slots.at[peer(mask)[1]], ssem.at[mask], rsem.at[mask])
        total = slots[0].astype(F32)
        for i in range(1, 8):
            total = total + slots[i].astype(F32)
        return total

    def planes_start(slots, ssem, rsem):
        for t in range(1, nz):
            send(slots.at[z], slots.at[z], ssem.at[t], rsem.at[z], plane(t)[0])

    def planes_sum(slots, ssem, rsem):
        for t in range(1, nz):
            pz = plane(t)[1]
            arrive(slots.at[pz], ssem.at[t], rsem.at[pz])
        total = slots[0].astype(F32)
        for i in range(1, nz):
            total = total + slots[i].astype(F32)
        return total

    r.zpw[z] = plane_sum(r.rpw, r.pw_s, r.pw_r).astype(BF)
    planes_start(r.zpw, r.pz_s, r.pz_r)

    def char_back(i, gain_sum):
        at = rows(i, 128)
        upstream = dot_t(r.kq[0, at, :], r.cwt[0])
        for hh in range(1, G):
            upstream = upstream + dot_t(r.kq[hh, at, :], r.cwt[hh])
        values = r.xin[pl.ds(i * 8, 8)].astype(F32).reshape(128, C)
        back, gain = rms_back(upstream, values, r.cg[...])
        of_word = jnp.broadcast_to(r.gsum[rows(i, 8), :][:, None, :], (8, L, C)).reshape(128, C)
        full = back + r.shc[at, 0:1] * of_word
        r.xin[pl.ds(i * 8, 8)] = full.astype(BF).reshape(8, L, C)
        return gain_sum + gain

    gain_char = lax.fori_loop(0, GROUPS, char_back, jnp.zeros((1, C), F32))
    st_chars = load(r.xin, r.o_chars, 20)
    r.gn[2:3, 256:512] = gain_char
    r.gn[3:8, :] = jnp.zeros((5, D), F32)
    for mask in range(1, 8):
        send(r.gn, r.rgn.at[p], r.gn_s.at[mask], r.gn_r.at[mask], peer(mask)[0])
    r.rgn[p] = r.gn[...]

    r.zcw[z] = plane_sum(r.rcw, r.cw_s, r.cw_r).astype(BF)
    planes_start(r.zcw, r.cz_s, r.cz_r)
    r.zgn[z] = plane_sum(r.rgn, r.gn_s, r.gn_r)
    planes_start(r.zgn, r.gz_s, r.gz_r)
    final_cross(r.o_ffn, FR // nz, r.fa_s, r.fa_r, st_ffn, 2)
    r.pfin[...] = planes_sum(r.zpw, r.pz_s, r.pz_r).astype(BF)
    for mask in range(1, 8):
        mine = r.o_pool.at[rows(p, 32)]
        send(r.pfin, mine, r.pa_s.at[mask], r.pa_r.at[mask], peer(mask)[0])
    st_pool = load(r.pfin, r.o_pool.at[rows(p, 32)], 21)
    final_cross(r.o_att, AR // nz, r.aa_s, r.aa_r, st_att, 3)
    r.cfin[...] = planes_sum(r.zcw, r.cz_s, r.cz_r).astype(BF)
    send(r.cfin, r.o_chr.at[x], r.x_s.at[4], r.x_r.at[4], peer(4)[0])
    st_chr = load(r.cfin, r.o_chr.at[x], 22)
    r.gnf[...] = planes_sum(r.zgn, r.gz_s, r.gz_r)
    st_gain = load(r.gnf, r.o_gain, 23)

    arrive(r.o_ffn.at[1 - x], r.x_s.at[2], r.x_r.at[2])
    arrive(r.o_att.at[1 - x], r.x_s.at[3], r.x_r.at[3])
    arrive(r.o_chr.at[1 - x], r.x_s.at[4], r.x_r.at[4])
    for mask in range(1, 8):
        arrive(r.o_pool.at[rows(peer(mask)[1], 32)], r.pa_s.at[mask], r.pa_r.at[mask])
    for mask in range(1, 4):
        from_head = peer(mask)[0][1]
        arrive(r.o_layer.at[rows(from_head, Q)], r.ly_s.at[mask], r.ly_r.at[mask])
        arrive(r.o_words.at[rows(from_head, Q)], r.gw_s.at[mask], r.gw_r.at[mask])
    for copy in (st_lay, st_gw, st_chars, st_pool, st_chr, st_gain):
        copy.wait()
    for copy in sends:
        copy.wait_send()
    for t in range(1, nz):
        @pl.when(z + t < nz)
        def _():
            docs_copy(t, z).wait_send()

    @pl.when(z + 1 < nz)
    def _():
        def sent(u, carry):
            unit_copy(u).wait_send()
            return carry

        lax.fori_loop(0, 2 * z + 2, sent, 0)

    def grads_sent(u, carry):
        grad_copy(u).wait_send()
        return carry

    lax.fori_loop(jnp.maximum(2 * z - SLOTS, 0), 2 * z, grads_sent, 0)


def per_device(nz, *arguments):
    given = dict(zip(INPUTS, arguments))
    for name in ("char_count", "document_ids"):
        given[name] = given[name].reshape(G, 128)
    for name in ("char_gain", "pool_gain", "attn_gain", "ffn_gain"):
        given[name] = given[name].reshape(1, -1)
    scratch = scratch_list(nz)
    any_space = pl.BlockSpec(memory_space=pl.ANY)
    out_shape = [
        jax.ShapeDtypeStruct((W, D), BF),
        jax.ShapeDtypeStruct((W, D), BF),
        jax.ShapeDtypeStruct((Q, L, C), BF),
        jax.ShapeDtypeStruct((2, FR, 256), BF),
        jax.ShapeDtypeStruct((2, AR, 256), BF),
        jax.ShapeDtypeStruct((2, 128, 256), BF),
        jax.ShapeDtypeStruct((C, D), BF),
        jax.ShapeDtypeStruct((8, D), F32),
    ]
    names = INPUTS + OUTPUTS + list(scratch)
    layer, words, chars, ffn, att, chr_grad, pool, gain = pl.pallas_call(
        functools.partial(layer_kernel, nz, names),
        out_shape=out_shape,
        in_specs=[any_space] * len(INPUTS),
        out_specs=[any_space] * len(OUTPUTS),
        scratch_shapes=list(scratch.values()),
        compiler_params=pltpu.CompilerParams(
            collective_id=0, has_side_effects=True, vmem_limit_bytes=62 << 20
        ),
    )(*[given[name] for name in INPUTS])

    ffn, att, chr_grad = ffn.astype(F32), att.astype(F32), chr_grad.astype(F32)
    grad_ffn_up = jnp.concatenate([ffn[0, :512], ffn[1, :512]], axis=1)
    grad_ffn_down = jnp.concatenate(
        [jnp.concatenate([ffn[i, 512:768], ffn[i, 768:1024]], axis=1) for i in range(2)], axis=0
    )
    both = lambda a, b: jnp.concatenate([att[0, :, a:b], att[1, :, a:b]], axis=1)
    grad_attn_proj = jnp.stack([both(0, 64), both(128, 192), both(192, 256)])
    grad_attn_out = both(64, 128).T
    merged = chr_grad.reshape(C, 256)
    grad_char_proj = jnp.stack([merged[:, 0:64], merged[:, 64:128], merged[:, 192:256]])
    grad_char_out = merged[:, 128:192].T
    return (
        layer, words, chars,
        gain[2, 256:512], grad_char_proj, grad_char_out,
        gain[2, 0:256], pool.astype(F32),
        gain[1], grad_attn_proj, grad_attn_out,
        gain[0], grad_ffn_up, grad_ffn_down,
    )


def solution(mesh):
    nz = mesh.shape["seq"] // 2
    placed = (
        P("seq", None),
        P("seq", None, None),
        P("seq"),
        P("seq"),
        P("seq", None),
        P(),
        P(None, None, "head"),
        P("head", None),
        P(),
        P(),
        P(),
        P(None, None, "head"),
        P("head", None),
        P(),
        P(None, "head"),
        P("head", None),
    )
    return jax.shard_map(
        functools.partial(per_device, nz),
        mesh=mesh,
        in_specs=placed,
        out_specs=(
            P("seq", None),
            P("seq", None),
            P(("seq", "head"), None, None),
            P(),
            P(None, None, "head"),
            P("head", None),
            P(),
            P(),
            P(),
            P(None, None, "head"),
            P("head", None),
            P(),
            P(None, "head"),
            P("head", None),
        ),
        check_vma=False,
    )
```

time: 874 us -> 213 us (0.24); the launches traced: 860 us -> 213 us
  waiting for transfers between devices: 585 us -> 0 us
  Pallas kernels: 0 us -> 197 us
  matrix products: 106 us -> 0 us
  blocking collectives: 44.4 us -> 0 us
  local copies, waits for them, and re-layouts: 50.8 us -> 9.35 us
  other arithmetic: 46.9 us -> 5.89 us
  between operations: 15.1 us -> 0.78 us
  loops' own time: 11 us -> 0 us
    psum x6 -> x0, waiting for transfers between devices: 452 us -> none  [the longest x1 171 us: per_device(): lax.psum(jnp.dot(active_low, ffn_down, preferred_element_type=jnp.float32...]
    pallas_call x0 -> x1, Pallas kernels: none -> 197 us  [per_device(): pl.pallas_call(functools.partial(layer_kernel, nz, names), out_shape=out_...]
    dot_general x32 -> x0, matrix products: 98.7 us -> none  [the longest x3 11.1 us: word_scores(): jnp.einsum('qhd,khd->hqk', query_split, key_split, preferred_element_type...]
    reduce_scatter x1 -> x0, waiting for transfers between devices: 89.8 us -> none  [per_device(): lax.psum_scatter(lax.fori_loop(0, words_dev * lax.axis_size('seq') // key...]
    all_gather x2 -> x0, waiting for transfers between devices: 41.6 us -> none  [the longest x1 29.1 us: per_device(): lax.all_gather(value_low, 'seq', axis=0, tiled=True)]
    all_gather x1 -> x0, blocking collectives: 25 us -> none  [per_device(): lax.all_gather(document_ids.astype(jnp.bfloat16), 'seq', axis=0, tiled=True)]
    reduce_sum x7 -> x0, other arithmetic: 20.3 us -> none  [the longest x3 10.4 us: rms_backward(): jnp.sum((upstream * normal).reshape(-1, normal.shape[-1]), axis=0)]
    psum x1 -> x0, blocking collectives: 19.4 us -> none  [per_device(): lax.psum((grad_char_gain, grad_char_proj, grad_char_out, grad_pool_gain,...]
  transfers between devices with their start and end apart: 9 -> 0, of which waited for: 9 -> 0; matrix products, arithmetic and copies ran while one was open for 6% -> 0% of each run, Pallas kernels for 0% -> 0%
where the time goes in v1:
time: 213 us
  Pallas kernels  197 us (92%)
  local copies, waits for them, and re-layouts  9.35 us (4%)
  other arithmetic  5.89 us (3%)
    pallas_call x1, Pallas kernels, per_device(): pl.pallas_call(functools.partial(layer_kernel, nz, names), out_shape=out_...  197 us
    unnamed x21, local copies, waits for them, and re-layouts  6.08 us

profile of v1, /device:TPU:12, one launch (start us, length us, event | category | flops | bytes accessed | tf_op | source)
XLA Modules:
  0.0 212.9 jit_solution(15139489144095417824)
XLA Ops:
  0.6 1.7 copy.30.refs_6_
  2.4 196.8 %shard_map.263 = (bf16[512,512]{1,0:T(8,128)(2,1)}, bf16[512,512]{1,0:T(8,128)(2,1)}, bf16[128,16,256]{2,1,0:T(8,128)(2,1)}, bf16[2,1024,256]{2,1,0:T(8,128)(2,1...) custom-call(bf16[512,512]{1,0:T(8,128)(2,1)} %refs_0_.1, ...), custom_call_target="tpu_custom_call" | custom-call | tf_op jit(solution)/shard_map/pallas_call | solution.py:1053
  199.2 1.1 convert_element_type.11
  200.3 0.3 slice_bitcast_fusion.7
  200.7 0.0 copy-start
  200.7 0.2 maximum_bitcast_fusion
  200.9 0.1 maximum_bitcast_fusion.2
  201.0 0.9 pad_maximum_fusion.1
  202.0 0.0 copy-done
  202.0 0.2 convert_element_type.12
  202.1 0.1 slice_bitcast_fusion.5
  202.2 0.1 slice_bitcast_fusion.1
  202.3 0.0 copy-start.5
  202.3 1.6 pad_maximum_fusion
  203.9 0.0 copy-start.4
  203.9 0.0 copy-done.5
  204.0 0.0 copy-start.3
  204.0 0.1 fusion
  204.1 0.1 copy.38
  204.2 0.0 copy-start.2
  204.2 0.1 copy.36
  204.3 0.1 copy.37
  204.4 0.7 pad_maximum_fusion.2
  205.1 0.0 copy-start.1
  205.1 0.1 maximum_bitcast_fusion.3
  205.2 0.8 copy.35
  206.1 0.7 copy.39
  206.8 1.4 fusion.1
  208.2 1.3 fusion.2
  209.4 0.0 copy-done.4
  209.4 0.9 convert_element_type.10
  210.3 0.0 copy-done.3
  210.3 0.8 copy.43
  211.1 0.0 copy-done.2
  211.1 0.8 copy.44
  211.9 0.0 copy-done.1
  211.9 1.0 copy.45
  (1 shorter events, 0.0 us)
Async XLA Ops:
  200.7 1.3 copy-start
  202.3 1.7 copy-start.5
  203.9 5.5 %copy-start.4 = (bf16[256,512]{1,0:T(8,128)(2,1)S(1)}, bf16[256,512]{1,0:T(8,128)(2,1)}, u32[]{:S(2)}) copy-start(bf16[256,512]{1,0:T(8,128)(2,1)} %get-tuple-element.27) | copy-start | bytes 786436
  204.0 6.3 %copy-start.3 = (bf16[512,512]{1,0:T(8,128)(2,1)S(1)}, bf16[512,512]{1,0:T(8,128)(2,1)}, u32[]{:S(2)}) copy-start(bf16[512,512]{1,0:T(8,128)(2,1)} %get-tuple-element.84) | copy-start | bytes 1572868
  204.2 6.9 %copy-start.2 = (bf16[512,512]{1,0:T(8,128)(2,1)S(1)}, bf16[512,512]{1,0:T(8,128)(2,1)}, u32[]{:S(2)}) copy-start(bf16[512,512]{1,0:T(8,128)(2,1)} %get-tuple-element.85) | copy-start | bytes 1572868
  205.1 6.8 %copy-start.1 = (bf16[128,16,256]{2,1,0:T(8,128)(2,1)S(1)}, bf16[128,16,256]{2,1,0:T(8,128)(2,1)}, u32[]{:S(2)}) copy-start(bf16[128,16,256]{2,1,0:T(8,128)(2,1)} %get-tuple-element.86) | copy-start | bytes 3145732

commit v2 on v1

--- a/solution.py
+++ b/solution.py
@@ -24,7 +24,6 @@
 R = Q * L
 FS = 512
 GROUPS = R // 128
-QT = 256
 KU = 512
 MARKS = 8
 SLOTS = 8
@@ -64,6 +63,18 @@
     return lax.dot_general(a, b, (((0,), (0,)), ((), ())), preferred_element_type=F32)
 
 
+def bdot(a, b):
+    return lax.dot_general(a, b, (((2,), (1,)), ((0,), (0,))), preferred_element_type=F32)
+
+
+def bdot_t(a, b):
+    return lax.dot_general(a, b, (((2,), (2,)), ((0,), (0,))), preferred_element_type=F32)
+
+
+def bdot_l(a, b):
+    return lax.dot_general(a, b, (((1,), (1,)), ((0,), (0,))), preferred_element_type=F32)
+
+
 def iota(shape, axis):
     return lax.broadcasted_iota(jnp.int32, shape, axis)
 
@@ -92,7 +103,7 @@
         xin=vm((Q, L, C), BF),
         cnt=vm((G, 128), jnp.int32),
         docs=vm((n, G, 128), jnp.int32),
-        cpr=vm((3, C, 64), BF),
+        cpr=vm((3, 64, C), BF),
         win=vm((Q, D), BF),
         ogp=vm((2, W, D), BF),
         cg=vm((1, C), F32),
@@ -112,7 +123,9 @@
         share=vm((GROUPS, 8, 128), F32),
         shc=vm((R, 128), F32),
         msel=vm((GROUPS, 16, 128), BF),
-        bias=vm((GROUPS, 128, 128), F32),
+        live=vm((GROUPS, 128, 128), BF),
+        took=vm((G if nz <= 8 else 1, R, 128), BF),
+        bias=vm((GROUPS, 128, 128), BF),
         kq=vm((G, R, 256), BF),
         pt=vm((G, GROUPS, 128, 128), BF),
         pooled=vm((G, Q, 128), F32),
@@ -126,36 +139,31 @@
         flow=vm((Q, D), BF),
         lay=vm((Q, D), BF),
         fsum=vm((Q, D), F32),
-        act=vm((G, Q, FS), BF),
         lsum=vm((Q, D), F32),
         gsec=vm((Q, D), F32),
         gb=vm((Q, D), BF),
         gw=vm((Q, D), BF),
         gsum=vm((Q, C), F32),
-        skv=vm((8, Q, 128), BF),
-        sq=vm((8, 64, 128), BF),
-        rq=vm((8, 64, 128), BF),
+        wsel=vm((D, 256), BF),
         kv=vm((nz * PW, 128), BF),
         marks=vm((min(n, MARKS) * KU, 128), BF),
         qd=vm((PW, 256), BF),
-        m=vm((PW, 128), F32),
-        l=vm((PW, 128), F32),
-        acc=vm((PW, 128), F32),
+        top=vm((8, PW), F32),
+        total=vm((8, PW), F32),
+        lse=vm((8, PW), F32),
+        delta=vm((8, PW), F32),
+        acct=vm((128, PW), F32),
+        out=vm((PW, 128), F32),
         ob=vm((PW, 128), BF),
-        lser=vm((PW // QT, 8, QT), F32),
-        dlr=vm((PW // QT, 8, QT), F32),
         smx=vm((8, 64, 128), BF),
         rmx=vm((8, 64, 128), BF),
         sgm=vm((8, 64, 128), BF),
         rgm=vm((8, 64, 128), BF),
         gz=vm((PW, 128), BF),
         xg=vm((PW, 128), BF),
-        acck=vm((KU, 128), F32),
-        accv=vm((KU, 128), F32),
-        dq=vm((PW, 128), F32),
         dkv=vm((PW, 128), F32),
         sdk=vm((min(n, SLOTS), KU, 128), BF),
-        rdk=vm((nz, 2, KU, 128), BF),
+        rdk=vm((n, KU, 128), BF),
         dqb=vm((PW, 128), BF),
         sdkv=vm((8, Q, 128), BF),
         rdkv=vm((8, Q, 128), BF),
@@ -185,12 +193,12 @@
         zgn=vm((nz, 8, D), F32),
         gnf=vm((8, D), F32),
         lsem=dma((24,)),
-        wg_s=dma((6, 3)),
-        wg_r=dma((6, 3)),
-        kv_s=dma((8,)),
-        kv_r=dma((8,)),
-        q_s=dma((8,)),
-        q_r=dma((8,)),
+        wg_s=dma((2, 3)),
+        wg_r=dma((2, 3)),
+        ws_s=dma((4, 5)),
+        ws_r=dma((4, 5)),
+        og_s=dma((2,)),
+        og_r=dma((2,)),
         mx_s=dma((8,)),
         mx_r=dma((8,)),
         gm_s=dma((8,)),
@@ -222,7 +230,11 @@
         x_s=dma((5,)),
         x_r=dma((5,)),
         dk_s=dma((n,)),
-        dk_r=dma((nz, 2)),
+        dk_r=dma((n,)),
+        xf_s=dma((nz,)),
+        xf_r=dma((nz,)),
+        xa_s=dma((nz,)),
+        xa_r=dma((nz,)),
         fr_s=dma((nz,)),
         fr_r=dma((nz,)),
         fa_s=dma((nz,)),
@@ -328,18 +340,18 @@
     place = (iota((64, 128), 0) == iota((64, 128), 1)).astype(F32).astype(BF)
     place_high = (iota((64, 128), 0) + 64 == iota((64, 128), 1)).astype(F32).astype(BF)
     wq, wk, wv = r.cpr[0], r.cpr[1], r.cpr[2]
-    r.cw[h, :, 0:128] = (dot(wk, place) + dot(wq, place_high)).astype(BF)
-    r.cw[h, :, 128:256] = (dot(wq, place) + dot(wv, place_high)).astype(BF)
+    r.cw[h, :, 0:128] = (dot_l(wk, place) + dot_l(wq, place_high)).astype(BF)
+    r.cw[h, :, 128:256] = (dot_l(wq, place) + dot_l(wv, place_high)).astype(BF)
 
     ld_x.wait()
     ld_cg.wait()
 
     def char_norm(i, carry):
-        values = r.xin[pl.ds(i * 8, 8)].astype(F32).reshape(128, C)
-        r.low[rows(i, 128), :] = (values * rms_factor(values) * r.cg[...]).astype(BF)
+        values = r.xin[pl.ds(i * 32, 32)].astype(F32).reshape(512, C)
+        r.low[rows(i, 512), :] = (values * rms_factor(values) * r.cg[...]).astype(BF)
         return carry
 
-    lax.fori_loop(0, GROUPS, char_norm, 0, unroll=2)
+    lax.fori_loop(0, R // 512, char_norm, 0)
 
     ld_cnt.wait()
     count_row = jnp.broadcast_to(r.cnt[pl.ds(h, 1), :].astype(F32), (128, 128))
@@ -362,11 +374,14 @@
         spread = jnp.where(lane == g * 8 + lax.div(row, L), 1.0, 0.0).astype(BF)
         count = dot(spread, r.cntm[...].astype(BF))
         valid = lax.rem(row, L).astype(F32) < count
-        r.bias[g] = jnp.where(valid & (lax.div(row, L) == lax.div(lane, L)), 0.0, NEGATIVE)
+        r.bias[g] = jnp.where(
+            valid & (lax.div(row, L) == lax.div(lane, L)), 0.0, NEGATIVE
+        ).astype(BF)
         r.shc[rows(g, 128), :] = jnp.where(valid, 1.0 / count, 0.0)
+        r.live[g] = jnp.where(valid, 1.0, 0.0).astype(BF)
         return carry
 
-    lax.fori_loop(0, GROUPS, char_masks, 0)
+    lax.fori_loop(0, GROUPS, char_masks, 0, unroll=4)
 
     pl.semaphore_wait(barrier, 7 + nz - 1)
 
@@ -386,58 +401,116 @@
     def gather_last(k, slots):
         arrive(slots(2 * (1 - y) + 1 - c), r.wg_s.at[k, 2], r.wg_r.at[k, 2])
 
+    def share_start(k, full, part):
+        send(full(h), full(h), r.ws_s.at[k, 0], r.ws_r.at[k, 0], peer(1)[0])
+        send(part(h, x), part(h, x), r.ws_s.at[k, 1], r.ws_r.at[k, 1], peer(2)[0])
+
+    def share_middle(k, full, part):
+        mine = part(2 * (1 - y) + c, x)
+        arrive(mine, r.ws_s.at[k, 1], r.ws_r.at[k, 1])
+        send(mine, mine, r.ws_s.at[k, 2], r.ws_r.at[k, 2], peer(4)[0])
+        send(mine, mine, r.ws_s.at[k, 3], r.ws_r.at[k, 3], peer(1)[0])
+
+    def share_end(k, full, part):
+        other = part(2 * (1 - y) + c, 1 - x)
+        arrive(other, r.ws_s.at[k, 2], r.ws_r.at[k, 2])
+        send(other, other, r.ws_s.at[k, 4], r.ws_r.at[k, 4], peer(1)[0])
+
+    def share_near(k, full, part):
+        arrive(full(2 * y + 1 - c), r.ws_s.at[k, 0], r.ws_r.at[k, 0])
+
+    def share_last(k, full, part):
+        far = 2 * (1 - y) + 1 - c
+        arrive(part(far, x), r.ws_s.at[k, 3], r.ws_r.at[k, 3])
+        arrive(part(far, 1 - x), r.ws_s.at[k, 4], r.ws_r.at[k, 4])
+
+    def fan_start(src, slots, ssem, rsem):
+        for mask in (1, 2, 4, 6):
+            send(src, slots.at[rows(p, Q)], ssem.at[mask], rsem.at[mask], peer(mask)[0])
+        slots[rows(p, Q), :] = src[...]
+
+    def fan_forward(slots, ssem, rsem):
+        for mask in (2, 4, 6):
+            got = slots.at[rows(peer(mask)[1], Q)]
+            arrive(got, ssem.at[mask], rsem.at[mask])
+            send(got, got, ssem.at[mask + 1], rsem.at[mask + 1], peer(1)[0])
+
+    def fan_last(slots, ssem, rsem):
+        for mask in (1, 3, 5, 7):
+            arrive(slots.at[rows(peer(mask)[1], Q)], ssem.at[mask], rsem.at[mask])
+
+    def head_rows_start(src, out, ssem, rsem):
+        for mask in (1, 2):
+            send(src, out.at[rows(h, Q)], ssem.at[mask], rsem.at[mask], peer(mask)[0])
+
+    def head_rows_forward(out, ssem, rsem):
+        got = out.at[rows(2 * (1 - y) + c, Q)]
+        arrive(got, ssem.at[2], rsem.at[2])
+        send(got, got, ssem.at[3], rsem.at[3], peer(1)[0])
+
+    def head_rows_last(out, ssem, rsem):
+        arrive(out.at[rows(2 * y + 1 - c, Q)], ssem.at[1], rsem.at[1])
+        arrive(out.at[rows(2 * (1 - y) + 1 - c, Q)], ssem.at[3], rsem.at[3])
+
     order = [h, 2 * y + 1 - c, 2 * (1 - y) + c, 2 * (1 - y) + 1 - c]
     cw_at = lambda i: r.cw.at[i]
     co_at = lambda i: r.co.at[i, pl.ds(64, 64)]
-    aw_at = lambda i: r.aw.at[i]
-    ao_at = lambda i: r.ao.at[i]
-    fu_at = lambda i: r.fu.at[i]
-    fd_at = lambda i: r.fd.at[i]
+    sh_aw = (0, lambda i: r.aw.at[i], lambda i, j: r.aw.at[i, :, rows(j, D // 2)])
+    sh_ao = (1, lambda i: r.ao.at[i], lambda i, j: r.ao.at[i, rows(j, 64)])
+    sh_fu = (2, lambda i: r.fu.at[i], lambda i, j: r.fu.at[i, rows(j, D // 2)])
+    sh_fd = (3, lambda i: r.fd.at[i], lambda i, j: r.fd.at[i, rows(j, FS // 2)])
 
     gather_start(0, cw_at)
     ld_co.wait()
     gather_start(1, co_at)
     ld_doc.wait()
     send(r.docs.at[s], r.docs.at[s], r.x_s.at[0], r.x_r.at[0], peer(4)[0])
-    ld_aw.wait()
-    gather_start(2, aw_at)
+    ld_ao.wait()
+    share_start(*sh_ao)
+    ld_fu.wait()
+    share_start(*sh_fu)
+    ld_og.wait()
+    og_half = lambda i, j: r.ogp.at[i, rows(j, W // 2)]
+    send(og_half(x, c), og_half(x, c), r.og_s.at[0], r.og_r.at[0], peer(4)[0])
 
     lane_scale = jnp.where((iota((1, 256), 1) < 64) | (iota((1, 256), 1) >= 192), 1.0, 0.125)
     keep_low = jnp.where(low_half, 1.0, 0.0)
     keep_high = 1.0 - keep_low
 
     def char_head(hh):
-        def project(i, carry):
-            got = dot(r.low[rows(i, 512), :], r.cw[hh]) * lane_scale
-            r.kq[hh, rows(i, 512), :] = got.astype(BF)
-            return carry
-
-        lax.fori_loop(0, R // 512, project, 0)
-
-        def attend(g, carry):
-            kq = r.kq[hh, rows(g, 128), 0:128]
-            qv = r.kq[hh, rows(g, 128), 128:256]
-            query = (qv.astype(F32) * keep_low).astype(BF)
-            scores = dot_t(kq, query) + r.bias[g]
-            raised = jnp.exp(scores - jnp.max(scores, axis=0, keepdims=True))
-            weights = (raised * (1.0 / jnp.sum(raised, axis=0, keepdims=True))).astype(BF)
-            r.pt[hh, g] = weights
-            taken = dot_t(r.msel[g], weights).astype(BF)
-            got = dot(taken, qv)[:8] * (1.0 / r.cntm[rows(g, 8), :])
-            r.pooled[hh, rows(g, 8), :] = got * keep_high
-            return carry
-
-        lax.fori_loop(0, GROUPS, attend, 0, unroll=4)
-
-    char_head(order[0])
+        for i in range(2):
+            part = pl.ds(i * (R // 2), R // 2)
+            r.kq[hh, part, :] = (dot(r.low[part, :], r.cw[hh]) * lane_scale).astype(BF)
+        kq = r.kq[hh, :, 0:128].reshape(GROUPS, 128, 128)
+        qv = r.kq[hh, :, 128:256].astype(F32)
+        query = (qv * keep_low).astype(BF).reshape(GROUPS, 128, 128)
+        scores = bdot_t(kq, query) + r.bias[...].astype(F32)
+        raised = jnp.exp(scores - jnp.max(scores, axis=1, keepdims=True))
+        weights = (raised * (1.0 / jnp.sum(raised, axis=1, keepdims=True))).astype(BF)
+        r.pt[hh] = weights
+        took = bdot(weights, r.live[...]).reshape(R, 128)
+        if nz <= 8:
+            r.took[hh] = took.astype(BF)
+        got = jnp.sum((took * qv).reshape(Q, L, 128), axis=1)
+        r.pooled[hh] = got * (1.0 / r.cntm[...]) * keep_high
+
+    ld_aw.wait()
+    first, other = r.aw[h, 0].astype(F32), r.aw[h, 1].astype(F32)
+    third = r.aw[h, 2].astype(F32)
+    even = x == 0
+    r.wsel[:, 0:128] = (jnp.where(even, first, swap(first)) * 0.125 * keep_low).astype(BF)
+    r.wsel[:, 128:256] = jnp.where(even, pick(other, swap(third)), pick(swap(other), third)).astype(BF)
+    char_head(h)
     gather_near(0, cw_at)
-    char_head(order[1])
     gather_forward(0, cw_at)
     gather_forward(1, co_at)
-    gather_forward(2, aw_at)
-    char_head(order[2])
     gather_last(0, cw_at)
-    char_head(order[3])
+
+    def other_head(t, carry):
+        char_head(lax.rem(h + t, G))
+        return carry
+
+    lax.fori_loop(1, G, other_head, 0)
 
     def char_mean(g, carry):
         block = r.xin[pl.ds(g * 8, 8)].reshape(128, C)
@@ -460,24 +533,10 @@
     r.hid[...] = hidden
     r.alow[...] = (hidden * rms_factor(hidden) * r.ag[...]).astype(BF)
 
-    gather_near(2, aw_at)
-    gather_last(2, aw_at)
-    kv_mine = lambda i: r.kv.at[rows(z * 8 + i, Q)]
-    for t in range(G):
-        hh = order[t]
-        query = dot(r.alow[...], r.aw[hh, 0]) * 0.125
-        key = dot(r.alow[...], r.aw[hh, 1])
-        value = dot(r.alow[...], r.aw[hh, 2])
-        r.skv[hh] = pick(key, swap(value)).astype(BF)
-        r.skv[4 + hh] = pick(swap(key), value).astype(BF)
-        r.sq[hh] = pack(query).astype(BF)
-        r.sq[4 + hh] = pack_high(query).astype(BF)
-        for mask in ((4,) if t == 0 else (t, t + 4)):
-            device, to = peer(mask)
-            send(r.skv.at[to], kv_mine(p), r.kv_s.at[mask], r.kv_r.at[mask], device)
-            send(r.sq.at[to], r.rq.at[p], r.q_s.at[mask], r.q_r.at[mask], device)
-    r.kv[rows(z * 8 + p, Q), :] = r.skv[p]
-    r.rq[p] = r.sq[p]
+    fan_start(r.alow, r.alp, r.al_s, r.al_r)
+    ld_fd.wait()
+    share_start(*sh_fd)
+    kv_mine = rows(z, PW)
 
     arrive(r.docs.at[2 * z + 1 - x], r.x_s.at[0], r.x_r.at[0])
     docs_mine = r.docs.at[pl.ds(2 * z, 2)]
@@ -510,12 +569,14 @@
 
     lax.fori_loop(z * 8, z * 8 + 8, key_marks, 0)
     lax.fori_loop(0, 8, query_marks, 0)
-    r.m[...] = jnp.full((PW, 128), NEGATIVE, F32)
-    r.l[...] = jnp.zeros((PW, 128), F32)
-    r.acc[...] = jnp.zeros((PW, 128), F32)
-
-    for mask in range(1, 8):
-        arrive(kv_mine(peer(mask)[1]), r.kv_s.at[mask], r.kv_r.at[mask])
+    r.top[...] = jnp.full((8, PW), NEGATIVE, F32)
+    r.total[...] = jnp.zeros((8, PW), F32)
+    r.acct[...] = jnp.zeros((128, PW), F32)
+    fan_forward(r.alp, r.al_s, r.al_r)
+    fan_last(r.alp, r.al_s, r.al_r)
+    mapped = dot(r.alp[...], r.wsel[...])
+    r.qd[:, 0:128] = mapped[:, 0:128].astype(BF)
+    r.kv[kv_mine, :] = mapped[:, 128:256].astype(BF)
 
     def unit_copy(u):
         block = r.kv.at[rows(u, KU)]
@@ -528,28 +589,11 @@
         unit_copy(2 * z).start()
         unit_copy(2 * z + 1).start()
 
-    for mask in range(1, 8):
-        arrive(r.rq.at[peer(mask)[1]], r.q_s.at[mask], r.q_r.at[mask])
-
-    def unpack_queries(i, carry):
-        got = r.rq[i].astype(F32)
-        r.qd[rows(2 * i, 64), 0:128] = (got * keep_low).astype(BF)
-        r.qd[rows(2 * i + 1, 64), 0:128] = (swap(got) * keep_low).astype(BF)
-        return carry
-
-    lax.fori_loop(0, 8, unpack_queries, 0)
-
-    ld_ao.wait()
-    gather_start(3, ao_at)
-    ld_fu.wait()
-    gather_start(4, fu_at)
-    ld_fd.wait()
-    gather_start(5, fd_at)
-    ld_og.wait()
-    send(r.ogp.at[x], r.ogp.at[x], r.x_s.at[1], r.x_r.at[1], peer(4)[0])
-    for mask in range(1, 8):
-        send(r.alow, r.alp.at[rows(p, Q)], r.al_s.at[mask], r.al_r.at[mask], peer(mask)[0])
-    r.alp[rows(p, Q), :] = r.alow[...]
+    share_middle(*sh_ao)
+    share_middle(*sh_fu)
+    share_end(*sh_ao)
+    arrive(og_half(1 - x, c), r.og_s.at[0], r.og_r.at[0])
+    send(og_half(1 - x, c), og_half(1 - x, c), r.og_s.at[1], r.og_r.at[1], peer(1)[0])
 
     def marked(kv, u):
         marks = r.marks[rows(lax.rem(u, min(2 * nz, MARKS)), KU), :]
@@ -559,31 +603,24 @@
         if 2 * nz > MARKS:
             lax.fori_loop(4 * u, 4 * u + 4, key_marks, 0)
 
-    def forward_tile(qt, u, causal):
-        at = rows(qt, QT)
+    def forward_tile(u, start, causal):
+        at = pl.ds(start, PW - start)
         kv = r.kv[rows(u, KU), :]
-        scores = dot_t(r.qd[at, :], marked(kv, u))
+        scores = dot_t(marked(kv, u), r.qd[at, :])
         if causal:
-            gap = (qt * QT - (u - 2 * z) * KU) + iota((QT, KU), 0) - iota((QT, KU), 1)
+            gap = iota(scores.shape, 1) - iota(scores.shape, 0)
             scores = jnp.where(gap >= 0, scores, NEGATIVE)
-        old = r.m[at, :]
-        new = jnp.maximum(old, jnp.max(scores, axis=1, keepdims=True))
-        raised = jnp.exp(scores - new[:, 0:1])
+        old = r.top[0:1, at]
+        new = jnp.maximum(old, jnp.max(scores, axis=0, keepdims=True))
+        raised = jnp.exp(scores - new)
         fade = jnp.exp(old - new)
-        r.m[at, :] = new
-        r.l[at, :] = r.l[at, :] * fade + jnp.sum(raised, axis=1, keepdims=True)
-        r.acc[at, :] = r.acc[at, :] * fade + dot(raised.astype(BF), kv)
-
-    def forward_first(qt, carry):
-        forward_tile(qt, 2 * z, True)
-        return carry
-
-    def forward_second(qt, carry):
-        forward_tile(qt, 2 * z + 1, True)
-        return carry
-
-    lax.fori_loop(0, PW // QT, forward_first, 0)
-    lax.fori_loop(KU // QT, PW // QT, forward_second, 0)
+        r.top[0:1, at] = new
+        r.total[0:1, at] = r.total[0:1, at] * fade + jnp.sum(raised, axis=0, keepdims=True)
+        turned = kv.astype(F32).T.astype(BF)
+        r.acct[:, at] = r.acct[:, at] * fade + dot(turned, raised.astype(BF))
+
+    forward_tile(2 * z, 0, True)
+    forward_tile(2 * z + 1, KU, True)
 
     def wait_docs(source, carry):
         docs_copy(1, source).wait_recv()
@@ -602,37 +639,29 @@
         def _():
             unit_copy(u).start()
 
-        def step(qt, inner):
-            forward_tile(qt, u, False)
-            return inner
-
-        return lax.fori_loop(0, PW // QT, step, carry)
-
-    lax.fori_loop(0, 2 * z, forward_unit, 0)
-
-    def finish_rows(qt, carry):
-        for half in range(2):
-            i = 2 * qt + half
-            at = rows(i, 128)
-            total = r.l[at, :]
-            out = r.acc[at, :] * (1.0 / total) * keep_high
-            r.acc[at, :] = out
-            r.ob[at, :] = out.astype(BF)
-            r.smx[i] = pack_high(out).astype(BF)
-            lse = (r.m[at, :] + jnp.log(total)).T
-            r.lser[qt, :, half * 128 : half * 128 + 128] = lse[:8]
+        forward_tile(u, 0, False)
         return carry
 
-    lax.fori_loop(0, PW // QT, finish_rows, 0)
+    lax.fori_loop(0, jnp.minimum(2 * z, 2), forward_unit, 0)
+    share_middle(*sh_fd)
+    share_end(*sh_fu)
+    lax.fori_loop(jnp.minimum(2 * z, 2), 2 * z, forward_unit, 0)
+    share_end(*sh_fd)
+
+    r.lse[0:1, :] = r.top[0:1, :] + jnp.log(r.total[0:1, :])
+    over = 1.0 / r.total[0:1, :]
+    for i in range(8):
+        cols = slice(i * 128, i * 128 + 128)
+        out = (r.acct[:, cols] * over[:, cols]).T * keep_high
+        r.out[cols, :] = out
+        r.ob[cols, :] = out.astype(BF)
+        r.smx[i] = pack_high(out).astype(BF)
     for mask in range(1, 8):
         device, to = peer(mask)
         send(r.smx.at[to], r.rmx.at[p], r.mx_s.at[mask], r.mx_r.at[mask], device)
     r.rmx[p] = r.smx[p]
-    gather_forward(3, ao_at)
-    gather_forward(4, fu_at)
-    gather_forward(5, fd_at)
-    gather_near(3, ao_at)
-    gather_last(3, ao_at)
+    share_near(*sh_ao)
+    share_last(*sh_ao)
     ld_fg.wait()
     for mask in range(1, 8):
         arrive(r.rmx.at[peer(mask)[1]], r.mx_s.at[mask], r.mx_r.at[mask])
@@ -647,16 +676,18 @@
     r.sec[...] = second
     r.flow[...] = (second * rms_factor(second) * r.fg[...]).astype(BF)
 
+    fan_start(r.flow, r.flp, r.fl_s, r.fl_r)
+
     grad_rows = r.ogp[x, rows(h, Q), :]
     r.fsum[...] = jnp.zeros((Q, D), F32)
     for t in range(G):
         hh = order[t]
         if t == 1:
-            gather_near(4, fu_at)
-            gather_near(5, fd_at)
+            share_near(*sh_fu)
+            share_near(*sh_fd)
         if t == 3:
-            gather_last(4, fu_at)
-            gather_last(5, fd_at)
+            share_last(*sh_fu)
+            share_last(*sh_fd)
         upward = dot(r.flow[...], r.fu[hh])
         square = upward * upward
         inner = 0.7978845608028654 * upward * (1.0 + 0.044715 * square)
@@ -666,7 +697,6 @@
         slope = half_up + 0.5 * upward * (1.0 - bent * bent) * (
             0.7978845608028654 * (1.0 + 0.134145 * square)
         )
-        r.act[hh] = active
         grad_up = (dot_t(grad_rows, r.fd[hh]) * slope).astype(BF)
         r.fsum[...] += dot_t(grad_up, r.fu[hh])
         r.sag[hh, :, 0:256] = active[:, 0:256]
@@ -688,11 +718,16 @@
             device, to = peer(mask)
             send(r.sgm.at[to], r.rgm.at[p], r.gm_s.at[mask], r.gm_r.at[mask], device)
     r.rgm[p] = r.sgm[p]
-    r.dq[...] = jnp.zeros((PW, 128), F32)
+    for mask in range(1, 8):
+        device, to = peer(mask)
+        send(r.sag.at[to], r.rag.at[rows(p, Q)], r.ac_s.at[mask], r.ac_r.at[mask], device)
+    r.rag[rows(p, Q), :] = r.sag[p]
+    r.acct[...] = jnp.zeros((128, PW), F32)
     r.lsum[...] = r.sec[...]
 
     def layer_part(hh, carry):
-        r.lsum[...] += dot(r.act[hh], r.fd[hh])
+        r.lsum[...] += dot(r.sag[hh, :, 0:256], r.fd[hh, 0:256, :])
+        r.lsum[...] += dot(r.sag[4 + hh, :, 0:256], r.fd[hh, 256:512, :])
         return carry
 
     lax.fori_loop(0, G, layer_part, 0)
@@ -700,95 +735,92 @@
     for mask in range(1, 8):
         arrive(r.rgm.at[peer(mask)[1]], r.gm_s.at[mask], r.gm_r.at[mask])
 
-    def unpack_grads(qt, carry):
-        for half in range(2):
-            i = 2 * qt + half
-            at = rows(i, 128)
-            got = r.rgm[i].astype(F32)
-            grad = jnp.concatenate([swap(got), got], axis=0) * keep_high
-            r.gz[at, :] = grad.astype(BF)
-            r.xg[at, :] = pick(r.qd[at, 0:128].astype(F32), grad).astype(BF)
-            delta = jnp.sum(grad * r.acc[at, :], axis=1, keepdims=True)
-            r.dlr[qt, :, half * 128 : half * 128 + 128] = jnp.broadcast_to(delta, (128, 128)).T[:8]
-        return carry
-
-    lax.fori_loop(0, PW // QT, unpack_grads, 0)
-
-    for mask in range(1, 8):
-        device, to = peer(mask)
-        send(r.sag.at[to], r.rag.at[rows(p, Q)], r.ac_s.at[mask], r.ac_r.at[mask], device)
-        send(r.flow, r.flp.at[rows(p, Q)], r.fl_s.at[mask], r.fl_r.at[mask], device)
-        send(r.gb, r.gbp.at[rows(p, Q)], r.gb_s.at[mask], r.gb_r.at[mask], device)
-    r.rag[rows(p, Q), :] = r.sag[p]
-    r.flp[rows(p, Q), :] = r.flow[...]
-    r.gbp[rows(p, Q), :] = r.gb[...]
-    for mask in range(1, 4):
-        mine = r.o_layer.at[rows(h, Q)]
-        send(r.lay, mine, r.ly_s.at[mask], r.ly_r.at[mask], peer(mask)[0])
+    for i in range(8):
+        cols = slice(i * 128, i * 128 + 128)
+        got = r.rgm[i].astype(F32)
+        grad = jnp.concatenate([swap(got), got], axis=0) * keep_high
+        r.gz[cols, :] = grad.astype(BF)
+        r.xg[cols, :] = pick(r.qd[cols, 0:128].astype(F32), grad).astype(BF)
+        r.delta[0:1, cols] = jnp.sum((grad * r.out[cols, :]).T, axis=0, keepdims=True)
+
+    fan_start(r.gb, r.gbp, r.gb_s, r.gb_r)
+    share_start(*sh_aw)
+    head_rows_start(r.lay, r.o_layer, r.ly_s, r.ly_r)
+    fan_forward(r.flp, r.fl_s, r.fl_r)
     st_lay = load(r.lay, r.o_layer.at[rows(h, Q)], 16)
 
-    def backward_tile(qt, u, causal):
-        at = rows(qt, QT)
+    def backward_tile(u, start, causal):
+        at = pl.ds(start, PW - start)
         kv = r.kv[rows(u, KU), :]
         scores = dot_t(marked(kv, u), r.qd[at, :])
-        weights = jnp.exp(scores - r.lser[qt, 0:1, :])
+        weights = jnp.exp(scores - r.lse[0:1, at])
         if causal:
-            gap = (qt * QT - (u - 2 * z) * KU) + iota((KU, QT), 1) - iota((KU, QT), 0)
+            gap = iota(scores.shape, 1) - iota(scores.shape, 0)
             weights = jnp.where(gap >= 0, weights, 0.0)
         dweights = dot_t(kv, r.gz[at, :])
-        dscores = (weights * (dweights - r.dlr[qt, 0:1, :])).astype(BF)
+        dscores = (weights * (dweights - r.delta[0:1, at])).astype(BF)
         other = r.xg[at, :]
-        r.acck[...] += dot(dscores, other)
-        r.accv[...] += dot(weights.astype(BF), other)
-        r.dq[at, :] += dot_l(dscores, kv)
-
-    def clear_unit():
-        r.acck[...] = jnp.zeros((KU, 128), F32)
-        r.accv[...] = jnp.zeros((KU, 128), F32)
+        turned = kv.astype(F32).T.astype(BF)
+        r.acct[:, at] += dot(turned, dscores)
+        return pick(dot(dscores, other), dot(weights.astype(BF), other))
+
+    last = 2 * nz <= SLOTS
+
+    def grad_slot(u):
+        return lax.rem(u, min(2 * nz, SLOTS))
 
     def grad_copy(u):
-        pz = lax.div(u, 2)
         return remote(
-            r.sdk.at[lax.rem(u, min(2 * nz, SLOTS))], r.rdk.at[z, lax.rem(u, 2)], r.dk_s.at[u], r.dk_r.at[z, lax.rem(u, 2)],
-            (2 * pz + x, h),
+            r.sdk.at[grad_slot(u)], r.rdk.at[u], r.dk_s.at[u], r.dk_r.at[u],
+            (2 * lax.rem(z + nz - 1, nz) + x, h),
         )
 
+    def grad_join(u):
+        arrive(r.rdk.at[u], r.dk_s.at[u], r.dk_r.at[u])
+        slot = grad_slot(u)
+        r.sdk[slot] = (r.sdk[slot].astype(F32) + r.rdk[u].astype(F32)).astype(BF)
+
     def backward_unit(u, carry):
-        clear_unit()
         mark_again(u)
-        if 2 * nz > SLOTS:
+        if not last:
             @pl.when(u >= SLOTS)
             def _():
                 grad_copy(u - SLOTS).wait_send()
-
-        def step(qt, inner):
-            backward_tile(qt, u, False)
-            return inner
-
-        lax.fori_loop(0, PW // QT, step, 0)
-        r.sdk[lax.rem(u, min(2 * nz, SLOTS))] = pick(r.acck[...], r.accv[...]).astype(BF)
+        r.sdk[grad_slot(u)] = backward_tile(u, 0, False).astype(BF)
+        if last:
+            @pl.when(z == nz - 1)
+            def _():
+                grad_copy(u).start()
+        else:
+            @pl.when(z < nz - 1)
+            def _():
+                grad_join(u)
+            grad_copy(u).start()
+        return carry
+
+    def pass_on(u, carry):
+        grad_join(u)
         grad_copy(u).start()
         return carry
 
     lax.fori_loop(0, 2 * z, backward_unit, 0)
-    for own in range(2):
-        clear_unit()
-        mark_again(2 * z + own)
-
-        def own_step(qt, carry):
-            backward_tile(qt, 2 * z + own, True)
-            return carry
-
-        lax.fori_loop(own * (KU // QT), PW // QT, own_step, 0)
-        r.dkv[own * KU : own * KU + KU, :] = pick(r.acck[...], r.accv[...])
+    if last:
+        lax.fori_loop(0, jnp.where(z < nz - 1, 2 * z, 0), pass_on, 0)
+
+    def own_units():
+        for own in range(2):
+            mark_again(2 * z + own)
+            r.dkv[own * KU : own * KU + KU, :] = backward_tile(2 * z + own, own * KU, True)
 
     def all_arrive(dst, ssem, rsem):
         for mask in range(1, 8):
             arrive(dst.at[rows(peer(mask)[1], Q)], ssem.at[mask], rsem.at[mask])
 
     all_arrive(r.rag, r.ac_s, r.ac_r)
-    all_arrive(r.flp, r.fl_s, r.fl_r)
-    arrive(r.ogp.at[1 - x], r.x_s.at[1], r.x_r.at[1])
+    fan_last(r.flp, r.fl_s, r.fl_r)
+    fan_forward(r.gbp, r.gb_s, r.gb_r)
+    head_rows_forward(r.o_layer, r.ly_s, r.ly_r)
+    arrive(og_half(1 - x, 1 - c), r.og_s.at[1], r.og_r.at[1])
     for i in range(2):
         r.fw[i * 256 : i * 256 + 256, :] = dot_l(
             r.flp[:, i * 256 : i * 256 + 256], r.rag[:, 256:512]
@@ -813,39 +845,41 @@
             total = total + slots[i].astype(F32)
         return total.astype(BF)
 
-    def final_start(src, out, size, ssem, rsem, lk):
+    def final_start(src, out, size, ssem, rsem, xs, xr, lk):
         mine = out.at[x, rows(z, size)]
         for t in range(1, nz):
             send(src, mine, ssem.at[t], rsem.at[z], plane(t)[0])
+        send(src, mine, xs.at[z], xr.at[z], peer(4)[0])
         return load(src, mine, lk)
 
-    def final_cross(out, size, ssem, rsem, copy, k):
-        copy.wait()
+    def final_cross(out, size, ssem, rsem, xs, xr):
         for t in range(1, nz):
             pz = plane(t)[1]
-            arrive(out.at[x, rows(pz, size)], ssem.at[t], rsem.at[pz])
-        send(out.at[x], out.at[x], r.x_s.at[k], r.x_r.at[k], peer(4)[0])
+            part = out.at[x, rows(pz, size)]
+            arrive(part, ssem.at[t], rsem.at[pz])
+            send(part, part, xs.at[pz], xr.at[pz], peer(4)[0])
+
+    def final_last(out, size, xs, xr):
+        for i in range(nz):
+            arrive(out.at[1 - x, rows(i, size)], xs.at[i], xr.at[i])
 
     spread_start(r.fw, FR // nz, r.frs, r.fr_s, r.fr_r)
 
-    def add_grads(pz, carry):
+    own_units()
+
+    @pl.when(z < nz - 1)
+    def _():
         for own in range(2):
-            part = r.rdk.at[pz, own]
-            remote(part, part, r.dk_s.at[own], r.dk_r.at[pz, own], peer(1)[0]).wait_recv()
-            r.dkv[own * KU : own * KU + KU, :] += r.rdk[pz, own].astype(F32)
-        return carry
-
-    lax.fori_loop(z + 1, nz, add_grads, 0)
-
-    def back_rows(i, carry):
-        at = rows(i, 128)
-        r.sdkv[i] = r.dkv[at, :].astype(BF)
-        grad = r.dq[at, :] * 0.125
+            u = 2 * z + own
+            arrive(r.rdk.at[u], r.dk_s.at[u], r.dk_r.at[u])
+            r.dkv[own * KU : own * KU + KU, :] += r.rdk[u].astype(F32)
+
+    for i in range(8):
+        cols = slice(i * 128, i * 128 + 128)
+        r.sdkv[i] = r.dkv[cols, :].astype(BF)
+        grad = r.acct[:, cols].T * 0.125
         r.sdq[i] = pack(grad).astype(BF)
-        r.dqb[at, :] = (grad * keep_low).astype(BF)
-        return carry
-
-    lax.fori_loop(0, 8, back_rows, 0)
+        r.dqb[cols, :] = (grad * keep_low).astype(BF)
     for mask in range(1, 8):
         device, to = peer(mask)
         send(r.sdkv.at[to], r.rdkv.at[p], r.dkv_s.at[mask], r.dkv_r.at[mask], device)
@@ -853,8 +887,8 @@
     r.rdkv[p] = r.sdkv[p]
     r.rdq[p] = r.sdq[p]
 
-    all_arrive(r.alp, r.al_s, r.al_r)
-    all_arrive(r.gbp, r.gb_s, r.gb_r)
+    fan_last(r.gbp, r.gb_s, r.gb_r)
+    share_middle(*sh_aw)
     for i in range(2):
         cols = slice(i * 256, i * 256 + 256)
         r.aw_g[cols, 0:128] = (
@@ -866,6 +900,10 @@
     for mask in range(1, 8):
         arrive(r.rdkv.at[peer(mask)[1]], r.dkv_s.at[mask], r.dkv_r.at[mask])
         arrive(r.rdq.at[peer(mask)[1]], r.dq_s.at[mask], r.dq_r.at[mask])
+
+    share_end(*sh_aw)
+    share_near(*sh_aw)
+    share_last(*sh_aw)
 
     attn_sum = jnp.zeros((Q, D), F32)
     for hh in range(G):
@@ -876,9 +914,7 @@
     back, gain_attn = rms_back(attn_sum, r.hid[...], r.ag[...])
     r.gw[...] = (r.gsec[...] + back).astype(BF)
     r.gn[1:2, :] = gain_attn
-    for mask in range(1, 4):
-        mine = r.o_words.at[rows(h, Q)]
-        send(r.gw, mine, r.gw_s.at[mask], r.gw_r.at[mask], peer(mask)[0])
+    head_rows_start(r.gw, r.o_words, r.gw_s, r.gw_r)
     st_gw = load(r.gw, r.o_words.at[rows(h, Q)], 17)
     grad_summary, gain_pool = rms_back(dot_t(r.gw[...], r.pw[...]), r.summ[...], r.pg[...])
     r.gsum[...] = grad_summary
@@ -891,7 +927,9 @@
     r.rpw[p] = r.spw[rows(p, 32), :]
 
     r.ffin[...] = spread_sum(r.fw, FR // nz, r.frs, r.fr_s, r.fr_r)
-    st_ffn = final_start(r.ffin, r.o_ffn, FR // nz, r.fa_s, r.fa_r, 18)
+    st_ffn = final_start(r.ffin, r.o_ffn, FR // nz, r.fa_s, r.fa_r, r.xf_s, r.xf_r, 18)
+
+    ones = jnp.ones((128, 128), BF)
 
     def char_head_back(hh):
         r.gp[hh] = dot_t(gs_low, r.co[hh])
@@ -899,31 +937,27 @@
         r.cwt[hh, :, 0:128] = swap(w[:, 0:128]).astype(BF)
         r.cwt[hh, :, 128:256] = (w[:, 128:256] * keep_high).astype(BF)
 
-        def attend(g, carry):
-            at = rows(g, 128)
-            kq = r.kq[hh, at, 0:128]
-            value = r.kq[hh, at, 128:256].astype(F32)
-            grad8 = r.gp[hh, rows(g, 8), :]
-            grad = jnp.broadcast_to(grad8[:, None, :], (8, L, 128)).reshape(128, 128)
-            weights = r.pt[hh, g].astype(F32)
-            share = r.share[g, 0:1, :]
-            gain = jnp.sum(value * grad, axis=1, keepdims=True)
-            lifted = weights * gain
-            centre = jnp.sum(lifted, axis=0, keepdims=True)
-            dscores = ((lifted - weights * centre) * share).astype(BF)
-            taken = jnp.sum(weights * share, axis=1, keepdims=True)
-            grads = pick(dot_l(dscores, kq) * 0.125, dot(dscores, kq))
-            r.kq[hh, at, 0:128] = grads.astype(BF)
-            r.kq[hh, at, 128:256] = (taken * grad).astype(BF)
-            return carry
-
-        lax.fori_loop(0, GROUPS, attend, 0, unroll=4)
+        kq = r.kq[hh, :, 0:128].reshape(GROUPS, 128, 128)
+        grad = jnp.broadcast_to(r.gp[hh][:, None, :], (Q, L, 128)).reshape(R, 128)
+        gain = dot((r.kq[hh, :, 128:256].astype(F32) * grad).astype(BF), ones)
+        gain = gain.reshape(GROUPS, 128, 128)
+        weights = r.pt[hh].astype(F32)
+        centre = jnp.sum(weights * gain, axis=1, keepdims=True)
+        dscores = ((gain - centre) * (weights * r.share[:, 0:1, :])).astype(BF)
+        dquery = (bdot_l(dscores, kq) * 0.125).reshape(R, 128)
+        dkey = bdot(dscores, kq).reshape(R, 128)
+        r.kq[hh, :, 0:128] = pick(dquery, dkey).astype(BF)
+        if nz <= 8:
+            took = r.took[hh].astype(F32)
+        else:
+            took = bdot(r.pt[hh], r.live[...]).reshape(R, 128)
+        r.kq[hh, :, 128:256] = (took * r.shc[...] * grad).astype(BF)
         term = dot_l(r.low[...], r.kq[hh])
         pooled = swap(r.pooled[hh]).astype(BF)
         r.scw[hh, :, 0:128] = term[:, 0:128].astype(BF)
         r.scw[hh, :, 128:256] = (term[:, 128:256] + dot_l(gs_low, pooled)).astype(BF)
 
-    for t in (3, 2, 1, 0):
+    def char_term(t):
         hh = order[t]
         char_head_back(hh)
         for mask in ((4,) if t == 0 else (t, t + 4)):
@@ -932,10 +966,6 @@
             send(
                 r.scw.at[hh, rows(px, 128)], r.rcw.at[p], r.cw_s.at[mask], r.cw_r.at[mask], device
             )
-    r.rcw[p] = r.scw[h, rows(x, 128), :]
-
-    r.afin[...] = spread_sum(r.aw_g, AR // nz, r.ars, r.ar_s, r.ar_r)
-    st_att = final_start(r.afin, r.o_att, AR // nz, r.aa_s, r.aa_r, 19)
 
     def plane_sum(slots, ssem, rsem):
         for mask in range(1, 8):
@@ -958,22 +988,39 @@
             total = total + slots[i].astype(F32)
         return total
 
+    char_term(3)
+
+    r.afin[...] = spread_sum(r.aw_g, AR // nz, r.ars, r.ar_s, r.ar_r)
+    st_att = final_start(r.afin, r.o_att, AR // nz, r.aa_s, r.aa_r, r.xa_s, r.xa_r, 19)
+    head_rows_forward(r.o_words, r.gw_s, r.gw_r)
+
+    char_term(2)
     r.zpw[z] = plane_sum(r.rpw, r.pw_s, r.pw_r).astype(BF)
     planes_start(r.zpw, r.pz_s, r.pz_r)
 
-    def char_back(i, gain_sum):
-        at = rows(i, 128)
-        upstream = dot_t(r.kq[0, at, :], r.cwt[0])
+    char_term(1)
+
+    char_term(0)
+    r.rcw[p] = r.scw[h, rows(x, 128), :]
+
+    def char_back(i):
+        part = pl.ds(i * (R // 2), R // 2)
+        words = pl.ds(i * (Q // 2), Q // 2)
+        upstream = dot_t(r.kq[0, part, :], r.cwt[0])
         for hh in range(1, G):
-            upstream = upstream + dot_t(r.kq[hh, at, :], r.cwt[hh])
-        values = r.xin[pl.ds(i * 8, 8)].astype(F32).reshape(128, C)
+            upstream = upstream + dot_t(r.kq[hh, part, :], r.cwt[hh])
+        values = r.xin[words].astype(F32).reshape(R // 2, C)
         back, gain = rms_back(upstream, values, r.cg[...])
-        of_word = jnp.broadcast_to(r.gsum[rows(i, 8), :][:, None, :], (8, L, C)).reshape(128, C)
-        full = back + r.shc[at, 0:1] * of_word
-        r.xin[pl.ds(i * 8, 8)] = full.astype(BF).reshape(8, L, C)
-        return gain_sum + gain
-
-    gain_char = lax.fori_loop(0, GROUPS, char_back, jnp.zeros((1, C), F32))
+        of_word = jnp.broadcast_to(r.gsum[words, :][:, None, :], (Q // 2, L, C))
+        full = back + r.shc[part, 0:1] * of_word.reshape(R // 2, C)
+        r.xin[words] = full.astype(BF).reshape(Q // 2, L, C)
+        return gain
+
+    gain_char = char_back(0)
+
+    r.zcw[z] = plane_sum(r.rcw, r.cw_s, r.cw_r).astype(BF)
+    planes_start(r.zcw, r.cz_s, r.cz_r)
+    gain_char = gain_char + char_back(1)
     st_chars = load(r.xin, r.o_chars, 20)
     r.gn[2:3, 256:512] = gain_char
     r.gn[3:8, :] = jnp.zeros((5, D), F32)
@@ -981,33 +1028,29 @@
         send(r.gn, r.rgn.at[p], r.gn_s.at[mask], r.gn_r.at[mask], peer(mask)[0])
     r.rgn[p] = r.gn[...]
 
-    r.zcw[z] = plane_sum(r.rcw, r.cw_s, r.cw_r).astype(BF)
-    planes_start(r.zcw, r.cz_s, r.cz_r)
-    r.zgn[z] = plane_sum(r.rgn, r.gn_s, r.gn_r)
-    planes_start(r.zgn, r.gz_s, r.gz_r)
-    final_cross(r.o_ffn, FR // nz, r.fa_s, r.fa_r, st_ffn, 2)
+    final_cross(r.o_att, AR // nz, r.aa_s, r.aa_r, r.xa_s, r.xa_r)
+    final_cross(r.o_ffn, FR // nz, r.fa_s, r.fa_r, r.xf_s, r.xf_r)
     r.pfin[...] = planes_sum(r.zpw, r.pz_s, r.pz_r).astype(BF)
     for mask in range(1, 8):
         mine = r.o_pool.at[rows(p, 32)]
         send(r.pfin, mine, r.pa_s.at[mask], r.pa_r.at[mask], peer(mask)[0])
     st_pool = load(r.pfin, r.o_pool.at[rows(p, 32)], 21)
-    final_cross(r.o_att, AR // nz, r.aa_s, r.aa_r, st_att, 3)
+    r.zgn[z] = plane_sum(r.rgn, r.gn_s, r.gn_r)
+    planes_start(r.zgn, r.gz_s, r.gz_r)
     r.cfin[...] = planes_sum(r.zcw, r.cz_s, r.cz_r).astype(BF)
     send(r.cfin, r.o_chr.at[x], r.x_s.at[4], r.x_r.at[4], peer(4)[0])
     st_chr = load(r.cfin, r.o_chr.at[x], 22)
     r.gnf[...] = planes_sum(r.zgn, r.gz_s, r.gz_r)
     st_gain = load(r.gnf, r.o_gain, 23)
 
-    arrive(r.o_ffn.at[1 - x], r.x_s.at[2], r.x_r.at[2])
-    arrive(r.o_att.at[1 - x], r.x_s.at[3], r.x_r.at[3])
+    final_last(r.o_ffn, FR // nz, r.xf_s, r.xf_r)
+    final_last(r.o_att, AR // nz, r.xa_s, r.xa_r)
     arrive(r.o_chr.at[1 - x], r.x_s.at[4], r.x_r.at[4])
     for mask in range(1, 8):
         arrive(r.o_pool.at[rows(peer(mask)[1], 32)], r.pa_s.at[mask], r.pa_r.at[mask])
-    for mask in range(1, 4):
-        from_head = peer(mask)[0][1]
-        arrive(r.o_layer.at[rows(from_head, Q)], r.ly_s.at[mask], r.ly_r.at[mask])
-        arrive(r.o_words.at[rows(from_head, Q)], r.gw_s.at[mask], r.gw_r.at[mask])
-    for copy in (st_lay, st_gw, st_chars, st_pool, st_chr, st_gain):
+    head_rows_last(r.o_layer, r.ly_s, r.ly_r)
+    head_rows_last(r.o_words, r.gw_s, r.gw_r)
+    for copy in (st_ffn, st_att, st_lay, st_gw, st_chars, st_pool, st_chr, st_gain):
         copy.wait()
     for copy in sends:
         copy.wait_send()
@@ -1035,6 +1078,7 @@
     given = dict(zip(INPUTS, arguments))
     for name in ("char_count", "document_ids"):
         given[name] = given[name].reshape(G, 128)
+    given["char_proj"] = jnp.swapaxes(given["char_proj"], 1, 2)
     for name in ("char_gain", "pool_gain", "attn_gain", "ffn_gain"):
         given[name] = given[name].reshape(1, -1)
     scratch = scratch_list(nz)
@@ -1061,24 +1105,95 @@
         ),
     )(*[given[name] for name in INPUTS])
 
-    ffn, att, chr_grad = ffn.astype(F32), att.astype(F32), chr_grad.astype(F32)
-    grad_ffn_up = jnp.concatenate([ffn[0, :512], ffn[1, :512]], axis=1)
-    grad_ffn_down = jnp.concatenate(
-        [jnp.concatenate([ffn[i, 512:768], ffn[i, 768:1024]], axis=1) for i in range(2)], axis=0
-    )
-    both = lambda a, b: jnp.concatenate([att[0, :, a:b], att[1, :, a:b]], axis=1)
-    grad_attn_proj = jnp.stack([both(0, 64), both(128, 192), both(192, 256)])
-    grad_attn_out = both(64, 128).T
-    merged = chr_grad.reshape(C, 256)
-    grad_char_proj = jnp.stack([merged[:, 0:64], merged[:, 64:128], merged[:, 192:256]])
-    grad_char_out = merged[:, 128:192].T
-    return (
-        layer, words, chars,
-        gain[2, 256:512], grad_char_proj, grad_char_out,
-        gain[2, 0:256], pool.astype(F32),
-        gain[1], grad_attn_proj, grad_attn_out,
-        gain[0], grad_ffn_up, grad_ffn_down,
-    )
+    grads = [
+        jax.ShapeDtypeStruct((W, D), BF),
+        jax.ShapeDtypeStruct((W, D), BF),
+        jax.ShapeDtypeStruct((Q, L, C), BF),
+        jax.ShapeDtypeStruct((1, C), F32),
+        jax.ShapeDtypeStruct((3, 64, C), F32),
+        jax.ShapeDtypeStruct((64, C), F32),
+        jax.ShapeDtypeStruct((1, C), F32),
+        jax.ShapeDtypeStruct((C, D), F32),
+        jax.ShapeDtypeStruct((1, D), F32),
+        jax.ShapeDtypeStruct((3, D, 128), F32),
+        jax.ShapeDtypeStruct((128, D), F32),
+        jax.ShapeDtypeStruct((1, D), F32),
+        jax.ShapeDtypeStruct((D, FS), F32),
+        jax.ShapeDtypeStruct((FS, D), F32),
+    ]
+    result = pl.pallas_call(
+        unpack_kernel,
+        out_shape=grads,
+        in_specs=[any_space] * len(out_shape),
+        out_specs=[any_space] * len(grads),
+        scratch_shapes=[pltpu.VMEM(a.shape, a.dtype) for a in out_shape + grads[3:]]
+        + [pltpu.SemaphoreType.DMA((len(out_shape),)), pltpu.SemaphoreType.DMA((len(grads),))],
+        compiler_params=pltpu.CompilerParams(vmem_limit_bytes=62 << 20),
+    )(layer, words, chars, ffn, att, chr_grad, pool, gain)
+    result = list(result)
+    result[4] = jnp.swapaxes(result[4], 1, 2)
+    for i in (3, 6, 8, 11):
+        result[i] = result[i].reshape(-1)
+    return tuple(result)
+
+
+def unpack_kernel(*refs):
+    given, out, held, made = refs[0:8], refs[8:22], refs[22:30], refs[30:41]
+    in_sem, out_sem = refs[41:]
+    ffn, att, chr_grad, pool, gain = held[3:]
+    loads = [pltpu.make_async_copy(given[i], held[i], in_sem.at[i]) for i in range(8)]
+    stores = [pltpu.make_async_copy(held[i], out[i], out_sem.at[i]) for i in range(3)]
+    stores += [pltpu.make_async_copy(made[i], out[3 + i], out_sem.at[3 + i]) for i in range(11)]
+    for i in (3, 4, 2, 0, 1, 6, 5, 7):
+        loads[i].start()
+    (g_char, g_proj, g_out, g_pool, g_pproj, g_attn, g_aproj, g_aout, g_ffn, g_up, g_down) = made
+
+    def pick(a, b):
+        return jnp.where(iota(a.shape, 1) < 64, a, b)
+
+    loads[3].wait()
+    for i in range(2):
+        cols = slice(i * 256, i * 256 + 256)
+        g_up[:, cols] = ffn[i, 0:512, :].astype(F32)
+        g_down[cols, 0:256] = ffn[i, 512:768, :].astype(F32)
+        g_down[cols, 256:512] = ffn[i, 768:1024, :].astype(F32)
+    stores[12].start()
+    stores[13].start()
+    for i in (2, 0, 1):
+        loads[i].wait()
+        stores[i].start()
+    loads[4].wait()
+    first, other = att[0, :, 0:128].astype(F32), att[1, :, 0:128].astype(F32)
+    g_aproj[0] = pick(first, swap(other))
+    g_aout[...] = pick(swap(first), other).T
+    first, other = att[0, :, 128:256].astype(F32), att[1, :, 128:256].astype(F32)
+    g_aproj[1] = pick(first, swap(other))
+    g_aproj[2] = pick(swap(first), other)
+    stores[9].start()
+    stores[10].start()
+    loads[6].wait()
+    g_pproj[...] = pool[...].astype(F32)
+    stores[7].start()
+    loads[5].wait()
+    for i in range(2):
+        cols = slice(i * 128, i * 128 + 128)
+        block = chr_grad[i].astype(F32)
+        first, other = block[:, 0:128].T, block[:, 128:256].T
+        g_proj[0, :, cols] = first[0:64]
+        g_proj[1, :, cols] = first[64:128]
+        g_out[:, cols] = other[0:64]
+        g_proj[2, :, cols] = other[64:128]
+    stores[4].start()
+    stores[5].start()
+    loads[7].wait()
+    g_ffn[...] = gain[0:1, :]
+    g_attn[...] = gain[1:2, :]
+    g_pool[...] = gain[2:3, 0:256]
+    g_char[...] = gain[2:3, 256:512]
+    for i in (3, 6, 8, 11):
+        stores[i].start()
+    for copy in stores:
+        copy.wait()
 
 
 def solution(mesh):

time: 213 us -> 146 us (0.69)
  Pallas kernels: 197 us -> 144 us
  local copies, waits for them, and re-layouts: 9.35 us -> 0 us
  other arithmetic: 5.89 us -> 0 us
    pallas_call x1, Pallas kernels: 197 us -> 140 us  [per_device(): pl.pallas_call(functools.partial(layer_kernel, nz, names), out_shape=out_...]
    unnamed x21 -> x0, local copies, waits for them, and re-layouts: 6.08 us -> none
    pallas_call x0 -> x1, Pallas kernels: none -> 4.06 us  [per_device(): pl.pallas_call(unpack_kernel, out_shape=grads, in_specs=[any_space] * len...]
    slice x3 -> x0, local copies, waits for them, and re-layouts: 2.79 us -> none  [the longest x1 1.38 us: per_device(): gain[0]]
where the time goes in v2:
time: 146 us; the launch traced here: 145 us
  Pallas kernels  144 us (99%)
    pallas_call x1, Pallas kernels, per_device(): pl.pallas_call(functools.partial(layer_kernel, nz, names), out_shape=out_...  140 us
    pallas_call x1, Pallas kernels, per_device(): pl.pallas_call(unpack_kernel, out_shape=grads, in_specs=[any_space] * len...  4.06 us

profile of v2, /device:TPU:12, one launch (start us, length us, event | category | flops | bytes accessed | tf_op | source)
XLA Modules:
  0.0 144.8 jit_solution(1284720728159863256)
XLA Ops:
  0.7 140.0 %shard_map.263 = (bf16[512,512]{1,0:T(8,128)(2,1)}, bf16[512,512]{1,0:T(8,128)(2,1)}, bf16[128,16,256]{2,1,0:T(8,128)(2,1)}, bf16[2,1024,256]{2,1,0:T(8,128)(2,1...) custom-call(bf16[512,512]{1,0:T(8,128)(2,1)} %refs_0_.1, ...), custom_call_target="tpu_custom_call" | custom-call | tf_op jit(solution)/shard_map/pallas_call | solution.py:1097
  140.6 4.1 %shard_map.264 = (bf16[512,512]{1,0:T(8,128)(2,1)}, bf16[512,512]{1,0:T(8,128)(2,1)}, bf16[128,16,256]{2,1,0:T(8,128)(2,1)}, f32[1,256]{1,0:T(1,128)}, f32[3,64,...) custom-call(bf16[512,512]{1,0:T(8,128)(2,1)} %get-tuple-element.36.r, ...), custom_call_target="tpu_custom_call" | custom-call | tf_op jit(solution)/shard_map/pallas_call | solution.py:1124

commit v3 on v2

--- a/solution.py
+++ b/solution.py
@@ -28,6 +28,7 @@
 MARKS = 8
 SLOTS = 8
 FR = 1024
+FEW = 8
 AR = 512
 
 INPUTS = [
@@ -124,7 +125,7 @@
         shc=vm((R, 128), F32),
         msel=vm((GROUPS, 16, 128), BF),
         live=vm((GROUPS, 128, 128), BF),
-        took=vm((G if nz <= 8 else 1, R, 128), BF),
+        took=vm((G if nz <= FEW else 1, R, 128), BF),
         bias=vm((GROUPS, 128, 128), BF),
         kq=vm((G, R, 256), BF),
         pt=vm((G, GROUPS, 128, 128), BF),
@@ -192,7 +193,13 @@
         rgn=vm((8, 8, D), F32),
         zgn=vm((nz, 8, D), F32),
         gnf=vm((8, D), F32),
-        lsem=dma((24,)),
+        v_layer=vm((W, D) if nz <= FEW else (16, 128), BF),
+        v_words=vm((W, D) if nz <= FEW else (16, 128), BF),
+        v_ffn=vm((2, FR, 256) if nz <= FEW else (16, 128), BF),
+        v_att=vm((2, AR, 256) if nz <= FEW else (16, 128), BF),
+        v_chr=vm((2, 128, 256) if nz <= FEW else (16, 128), BF),
+        v_pool=vm((C, D) if nz <= FEW else (16, 128), BF),
+        lsem=dma((32,)),
         wg_s=dma((2, 3)),
         wg_r=dma((2, 3)),
         ws_s=dma((4, 5)),
@@ -299,6 +306,17 @@
         copy.start()
         return copy
 
+    few = nz <= FEW
+    land = {}
+    for name in ("layer", "words", "ffn", "att", "chr", "pool"):
+        land[name] = getattr(r, ("v_" if few else "o_") + name)
+
+    def keep_own(src, place, at, k):
+        if few:
+            place[at] = src[...]
+            return None
+        return load(src, place.at[at], k)
+
     low_half = iota((1, 128), 1) < 64
 
     def pick(a, b):
@@ -489,7 +507,7 @@
         weights = (raised * (1.0 / jnp.sum(raised, axis=1, keepdims=True))).astype(BF)
         r.pt[hh] = weights
         took = bdot(weights, r.live[...]).reshape(R, 128)
-        if nz <= 8:
+        if nz <= FEW:
             r.took[hh] = took.astype(BF)
         got = jnp.sum((took * qv).reshape(Q, L, 128), axis=1)
         r.pooled[hh] = got * (1.0 / r.cntm[...]) * keep_high
@@ -536,6 +554,9 @@
     fan_start(r.alow, r.alp, r.al_s, r.al_r)
     ld_fd.wait()
     share_start(*sh_fd)
+    share_start(*sh_aw)
+    share_middle(*sh_ao)
+    share_middle(*sh_fu)
     kv_mine = rows(z, PW)
 
     arrive(r.docs.at[2 * z + 1 - x], r.x_s.at[0], r.x_r.at[0])
@@ -589,9 +610,6 @@
         unit_copy(2 * z).start()
         unit_copy(2 * z + 1).start()
 
-    share_middle(*sh_ao)
-    share_middle(*sh_fu)
-    share_end(*sh_ao)
     arrive(og_half(1 - x, c), r.og_s.at[0], r.og_r.at[0])
     send(og_half(1 - x, c), og_half(1 - x, c), r.og_s.at[1], r.og_r.at[1], peer(1)[0])
 
@@ -621,6 +639,9 @@
 
     forward_tile(2 * z, 0, True)
     forward_tile(2 * z + 1, KU, True)
+    share_end(*sh_ao)
+    share_middle(*sh_fd)
+    share_end(*sh_fu)
 
     def wait_docs(source, carry):
         docs_copy(1, source).wait_recv()
@@ -643,10 +664,9 @@
         return carry
 
     lax.fori_loop(0, jnp.minimum(2 * z, 2), forward_unit, 0)
-    share_middle(*sh_fd)
-    share_end(*sh_fu)
+    share_end(*sh_fd)
+    share_middle(*sh_aw)
     lax.fori_loop(jnp.minimum(2 * z, 2), 2 * z, forward_unit, 0)
-    share_end(*sh_fd)
 
     r.lse[0:1, :] = r.top[0:1, :] + jnp.log(r.total[0:1, :])
     over = 1.0 / r.total[0:1, :]
@@ -660,6 +680,7 @@
         device, to = peer(mask)
         send(r.smx.at[to], r.rmx.at[p], r.mx_s.at[mask], r.mx_r.at[mask], device)
     r.rmx[p] = r.smx[p]
+    share_end(*sh_aw)
     share_near(*sh_ao)
     share_last(*sh_ao)
     ld_fg.wait()
@@ -744,10 +765,9 @@
         r.delta[0:1, cols] = jnp.sum((grad * r.out[cols, :]).T, axis=0, keepdims=True)
 
     fan_start(r.gb, r.gbp, r.gb_s, r.gb_r)
-    share_start(*sh_aw)
-    head_rows_start(r.lay, r.o_layer, r.ly_s, r.ly_r)
+    head_rows_start(r.lay, land["layer"], r.ly_s, r.ly_r)
     fan_forward(r.flp, r.fl_s, r.fl_r)
-    st_lay = load(r.lay, r.o_layer.at[rows(h, Q)], 16)
+    st_lay = keep_own(r.lay, land["layer"], (rows(h, Q), slice(None)), 16)
 
     def backward_tile(u, start, causal):
         at = pl.ds(start, PW - start)
@@ -812,14 +832,55 @@
             mark_again(2 * z + own)
             r.dkv[own * KU : own * KU + KU, :] = backward_tile(2 * z + own, own * KU, True)
 
+    own_units()
+
+    def spread_copy(src, size, slots, ssem, rsem, t):
+        device, pz = plane(t)
+        return remote(src.at[rows(pz, size)], slots.at[z], ssem.at[t], rsem.at[z], device)
+
+    def spread_start(src, size, slots, ssem, rsem, later):
+        for t in range(1, nz):
+            @pl.when((z + t < nz) if later else (z + t >= nz))
+            def _():
+                spread_copy(src, size, slots, ssem, rsem, t).start()
+        if not later:
+            for t in range(1, nz):
+                sends.append(spread_copy(src, size, slots, ssem, rsem, t))
+
     def all_arrive(dst, ssem, rsem):
         for mask in range(1, 8):
             arrive(dst.at[rows(peer(mask)[1], Q)], ssem.at[mask], rsem.at[mask])
 
+    def spread_sum(src, size, slots, ssem, rsem):
+        slots[z] = src[rows(z, size), :]
+        for t in range(1, nz):
+            pz = plane(t)[1]
+            arrive(slots.at[pz], ssem.at[t], rsem.at[pz])
+        total = slots[0].astype(F32)
+        for i in range(1, nz):
+            total = total + slots[i].astype(F32)
+        return total.astype(BF)
+
+    def final_start(src, out, size, ssem, rsem, xs, xr, lk):
+        mine = out.at[x, rows(z, size)]
+        for t in range(1, nz):
+            send(src, mine, ssem.at[t], rsem.at[z], plane(t)[0])
+        send(src, mine, xs.at[z], xr.at[z], peer(4)[0])
+        return keep_own(src, out, (x, rows(z, size)), lk)
+
+    def final_cross(out, size, ssem, rsem, xs, xr):
+        for t in range(1, nz):
+            pz = plane(t)[1]
+            part = out.at[x, rows(pz, size)]
+            arrive(part, ssem.at[t], rsem.at[pz])
+            send(part, part, xs.at[pz], xr.at[pz], peer(4)[0])
+
+    def final_last(out, size, xs, xr):
+        for i in range(nz):
+            arrive(out.at[1 - x, rows(i, size)], xs.at[i], xr.at[i])
+
     all_arrive(r.rag, r.ac_s, r.ac_r)
     fan_last(r.flp, r.fl_s, r.fl_r)
-    fan_forward(r.gbp, r.gb_s, r.gb_r)
-    head_rows_forward(r.o_layer, r.ly_s, r.ly_r)
     arrive(og_half(1 - x, 1 - c), r.og_s.at[1], r.og_r.at[1])
     for i in range(2):
         r.fw[i * 256 : i * 256 + 256, :] = dot_l(
@@ -830,42 +891,8 @@
             + dot_l(r.rag[W:PW, 0:256], r.ogp[1, :, i * 256 : i * 256 + 256])
         ).astype(BF)
 
-    def spread_start(src, size, slots, ssem, rsem):
-        for t in range(1, nz):
-            device, pz = plane(t)
-            send(src.at[rows(pz, size)], slots.at[z], ssem.at[t], rsem.at[z], device)
-
-    def spread_sum(src, size, slots, ssem, rsem):
-        slots[z] = src[rows(z, size), :]
-        for t in range(1, nz):
-            pz = plane(t)[1]
-            arrive(slots.at[pz], ssem.at[t], rsem.at[pz])
-        total = slots[0].astype(F32)
-        for i in range(1, nz):
-            total = total + slots[i].astype(F32)
-        return total.astype(BF)
-
-    def final_start(src, out, size, ssem, rsem, xs, xr, lk):
-        mine = out.at[x, rows(z, size)]
-        for t in range(1, nz):
-            send(src, mine, ssem.at[t], rsem.at[z], plane(t)[0])
-        send(src, mine, xs.at[z], xr.at[z], peer(4)[0])
-        return load(src, mine, lk)
-
-    def final_cross(out, size, ssem, rsem, xs, xr):
-        for t in range(1, nz):
-            pz = plane(t)[1]
-            part = out.at[x, rows(pz, size)]
-            arrive(part, ssem.at[t], rsem.at[pz])
-            send(part, part, xs.at[pz], xr.at[pz], peer(4)[0])
-
-    def final_last(out, size, xs, xr):
-        for i in range(nz):
-            arrive(out.at[1 - x, rows(i, size)], xs.at[i], xr.at[i])
-
-    spread_start(r.fw, FR // nz, r.frs, r.fr_s, r.fr_r)
-
-    own_units()
+    spread_start(r.fw, FR // nz, r.frs, r.fr_s, r.fr_r, True)
+    spread_start(r.fw, FR // nz, r.frs, r.fr_s, r.fr_r, False)
 
     @pl.when(z < nz - 1)
     def _():
@@ -887,21 +914,23 @@
     r.rdkv[p] = r.sdkv[p]
     r.rdq[p] = r.sdq[p]
 
+
+    fan_forward(r.gbp, r.gb_s, r.gb_r)
+    head_rows_forward(land["layer"], r.ly_s, r.ly_r)
     fan_last(r.gbp, r.gb_s, r.gb_r)
-    share_middle(*sh_aw)
     for i in range(2):
         cols = slice(i * 256, i * 256 + 256)
         r.aw_g[cols, 0:128] = (
             dot_l(r.alp[:, cols], r.dqb[...]) + dot_l(r.gbp[:, cols], r.ob[...])
         ).astype(BF)
         r.aw_g[cols, 128:256] = dot_l(r.alp[:, cols], r.sdkv[...].reshape(PW, 128)).astype(BF)
-    spread_start(r.aw_g, AR // nz, r.ars, r.ar_s, r.ar_r)
-
+
+    spread_start(r.aw_g, AR // nz, r.ars, r.ar_s, r.ar_r, True)
+    spread_start(r.aw_g, AR // nz, r.ars, r.ar_s, r.ar_r, False)
     for mask in range(1, 8):
         arrive(r.rdkv.at[peer(mask)[1]], r.dkv_s.at[mask], r.dkv_r.at[mask])
         arrive(r.rdq.at[peer(mask)[1]], r.dq_s.at[mask], r.dq_r.at[mask])
 
-    share_end(*sh_aw)
     share_near(*sh_aw)
     share_last(*sh_aw)
 
@@ -914,8 +943,8 @@
     back, gain_attn = rms_back(attn_sum, r.hid[...], r.ag[...])
     r.gw[...] = (r.gsec[...] + back).astype(BF)
     r.gn[1:2, :] = gain_attn
-    head_rows_start(r.gw, r.o_words, r.gw_s, r.gw_r)
-    st_gw = load(r.gw, r.o_words.at[rows(h, Q)], 17)
+    head_rows_start(r.gw, land["words"], r.gw_s, r.gw_r)
+    st_gw = keep_own(r.gw, land["words"], (rows(h, Q), slice(None)), 17)
     grad_summary, gain_pool = rms_back(dot_t(r.gw[...], r.pw[...]), r.summ[...], r.pg[...])
     r.gsum[...] = grad_summary
     gs_low = grad_summary.astype(BF)
@@ -925,9 +954,6 @@
         device, to = peer(mask)
         send(r.spw.at[rows(to, 32)], r.rpw.at[p], r.pw_s.at[mask], r.pw_r.at[mask], device)
     r.rpw[p] = r.spw[rows(p, 32), :]
-
-    r.ffin[...] = spread_sum(r.fw, FR // nz, r.frs, r.fr_s, r.fr_r)
-    st_ffn = final_start(r.ffin, r.o_ffn, FR // nz, r.fa_s, r.fa_r, r.xf_s, r.xf_r, 18)
 
     ones = jnp.ones((128, 128), BF)
 
@@ -947,7 +973,7 @@
         dquery = (bdot_l(dscores, kq) * 0.125).reshape(R, 128)
         dkey = bdot(dscores, kq).reshape(R, 128)
         r.kq[hh, :, 0:128] = pick(dquery, dkey).astype(BF)
-        if nz <= 8:
+        if nz <= FEW:
             took = r.took[hh].astype(F32)
         else:
             took = bdot(r.pt[hh], r.live[...]).reshape(R, 128)
@@ -989,19 +1015,17 @@
         return total
 
     char_term(3)
-
-    r.afin[...] = spread_sum(r.aw_g, AR // nz, r.ars, r.ar_s, r.ar_r)
-    st_att = final_start(r.afin, r.o_att, AR // nz, r.aa_s, r.aa_r, r.xa_s, r.xa_r, 19)
-    head_rows_forward(r.o_words, r.gw_s, r.gw_r)
-
     char_term(2)
+
+    r.ffin[...] = spread_sum(r.fw, FR // nz, r.frs, r.fr_s, r.fr_r)
+    st_ffn = final_start(r.ffin, land["ffn"], FR // nz, r.fa_s, r.fa_r, r.xf_s, r.xf_r, 18)
+    head_rows_forward(land["words"], r.gw_s, r.gw_r)
+
+    char_term(1)
+    char_term(0)
+    r.rcw[p] = r.scw[h, rows(x, 128), :]
     r.zpw[z] = plane_sum(r.rpw, r.pw_s, r.pw_r).astype(BF)
     planes_start(r.zpw, r.pz_s, r.pz_r)
-
-    char_term(1)
-
-    char_term(0)
-    r.rcw[p] = r.scw[h, rows(x, 128), :]
 
     def char_back(i):
         part = pl.ds(i * (R // 2), R // 2)
@@ -1018,6 +1042,10 @@
 
     gain_char = char_back(0)
 
+
+    r.afin[...] = spread_sum(r.aw_g, AR // nz, r.ars, r.ar_s, r.ar_r)
+    st_att = final_start(r.afin, land["att"], AR // nz, r.aa_s, r.aa_r, r.xa_s, r.xa_r, 19)
+
     r.zcw[z] = plane_sum(r.rcw, r.cw_s, r.cw_r).astype(BF)
     planes_start(r.zcw, r.cz_s, r.cz_r)
     gain_char = gain_char + char_back(1)
@@ -1028,30 +1056,43 @@
         send(r.gn, r.rgn.at[p], r.gn_s.at[mask], r.gn_r.at[mask], peer(mask)[0])
     r.rgn[p] = r.gn[...]
 
-    final_cross(r.o_att, AR // nz, r.aa_s, r.aa_r, r.xa_s, r.xa_r)
-    final_cross(r.o_ffn, FR // nz, r.fa_s, r.fa_r, r.xf_s, r.xf_r)
+    final_cross(land["ffn"], FR // nz, r.fa_s, r.fa_r, r.xf_s, r.xf_r)
+    final_cross(land["att"], AR // nz, r.aa_s, r.aa_r, r.xa_s, r.xa_r)
     r.pfin[...] = planes_sum(r.zpw, r.pz_s, r.pz_r).astype(BF)
     for mask in range(1, 8):
-        mine = r.o_pool.at[rows(p, 32)]
+        mine = land["pool"].at[rows(p, 32)]
         send(r.pfin, mine, r.pa_s.at[mask], r.pa_r.at[mask], peer(mask)[0])
-    st_pool = load(r.pfin, r.o_pool.at[rows(p, 32)], 21)
+    st_pool = keep_own(r.pfin, land["pool"], (rows(p, 32), slice(None)), 21)
     r.zgn[z] = plane_sum(r.rgn, r.gn_s, r.gn_r)
     planes_start(r.zgn, r.gz_s, r.gz_r)
     r.cfin[...] = planes_sum(r.zcw, r.cz_s, r.cz_r).astype(BF)
-    send(r.cfin, r.o_chr.at[x], r.x_s.at[4], r.x_r.at[4], peer(4)[0])
-    st_chr = load(r.cfin, r.o_chr.at[x], 22)
+    send(r.cfin, land["chr"].at[x], r.x_s.at[4], r.x_r.at[4], peer(4)[0])
+    st_chr = keep_own(r.cfin, land["chr"], x, 22)
     r.gnf[...] = planes_sum(r.zgn, r.gz_s, r.gz_r)
     st_gain = load(r.gnf, r.o_gain, 23)
 
-    final_last(r.o_ffn, FR // nz, r.xf_s, r.xf_r)
-    final_last(r.o_att, AR // nz, r.xa_s, r.xa_r)
-    arrive(r.o_chr.at[1 - x], r.x_s.at[4], r.x_r.at[4])
+    waiting = [st_chars, st_gain, st_ffn, st_att, st_lay, st_gw, st_pool, st_chr]
+
+    def finish(name, k):
+        if few:
+            waiting.append(load(land[name], getattr(r, "o_" + name), k))
+
+    head_rows_last(land["layer"], r.ly_s, r.ly_r)
+    finish("layer", 24)
+    head_rows_last(land["words"], r.gw_s, r.gw_r)
+    finish("words", 25)
+    final_last(land["ffn"], FR // nz, r.xf_s, r.xf_r)
+    finish("ffn", 26)
+    final_last(land["att"], AR // nz, r.xa_s, r.xa_r)
+    finish("att", 27)
     for mask in range(1, 8):
-        arrive(r.o_pool.at[rows(peer(mask)[1], 32)], r.pa_s.at[mask], r.pa_r.at[mask])
-    head_rows_last(r.o_layer, r.ly_s, r.ly_r)
-    head_rows_last(r.o_words, r.gw_s, r.gw_r)
-    for copy in (st_ffn, st_att, st_lay, st_gw, st_chars, st_pool, st_chr, st_gain):
-        copy.wait()
+        arrive(land["pool"].at[rows(peer(mask)[1], 32)], r.pa_s.at[mask], r.pa_r.at[mask])
+    finish("pool", 28)
+    arrive(land["chr"].at[1 - x], r.x_s.at[4], r.x_r.at[4])
+    finish("chr", 29)
+    for copy in waiting:
+        if copy is not None:
+            copy.wait()
     for copy in sends:
         copy.wait_send()
     for t in range(1, nz):

time: 146 us -> 143 us (0.979)
  Pallas kernels: 144 us -> 142 us
    pallas_call x1, Pallas kernels: 140 us -> 138 us  [per_device(): pl.pallas_call(functools.partial(layer_kernel, nz, names), out_shape=out_...]
where the time goes in v3:
time: 143 us; the launch traced here: 142 us
  Pallas kernels  142 us (99%)
    pallas_call x1, Pallas kernels, per_device(): pl.pallas_call(functools.partial(layer_kernel, nz, names), out_shape=out_...  138 us
    pallas_call x1, Pallas kernels, per_device(): pl.pallas_call(unpack_kernel, out_shape=grads, in_specs=[any_space] * len...  4.06 us

profile of v3, /device:TPU:12, one launch (start us, length us, event | category | flops | bytes accessed | tf_op | source)
XLA Modules:
  0.0 142.5 jit_solution(12642467682009469054)
XLA Ops:
  0.7 137.6 %shard_map.263 = (bf16[512,512]{1,0:T(8,128)(2,1)}, bf16[512,512]{1,0:T(8,128)(2,1)}, bf16[128,16,256]{2,1,0:T(8,128)(2,1)}, bf16[2,1024,256]{2,1,0:T(8,128)(2,1...) custom-call(bf16[512,512]{1,0:T(8,128)(2,1)} %refs_0_.1, ...), custom_call_target="tpu_custom_call" | custom-call | tf_op jit(solution)/shard_map/pallas_call | solution.py:1138
  138.2 4.1 %shard_map.264 = (bf16[512,512]{1,0:T(8,128)(2,1)}, bf16[512,512]{1,0:T(8,128)(2,1)}, bf16[128,16,256]{2,1,0:T(8,128)(2,1)}, f32[1,256]{1,0:T(1,128)}, f32[3,64,...) custom-call(bf16[512,512]{1,0:T(8,128)(2,1)} %get-tuple-element.36.r, ...), custom_call_target="tpu_custom_call" | custom-call | tf_op jit(solution)/shard_map/pallas_call | solution.py:1165

commit v4 on v3

--- a/solution.py
+++ b/solution.py
@@ -834,6 +834,16 @@
 
     own_units()
 
+    for i in range(8):
+        cols = slice(i * 128, i * 128 + 128)
+        grad = r.acct[:, cols].T * 0.125
+        r.sdq[i] = pack(grad).astype(BF)
+        r.dqb[cols, :] = (grad * keep_low).astype(BF)
+    for mask in range(1, 8):
+        device, to = peer(mask)
+        send(r.sdq.at[to], r.rdq.at[p], r.dq_s.at[mask], r.dq_r.at[mask], device)
+    r.rdq[p] = r.sdq[p]
+
     def spread_copy(src, size, slots, ssem, rsem, t):
         device, pz = plane(t)
         return remote(src.at[rows(pz, size)], slots.at[z], ssem.at[t], rsem.at[z], device)
@@ -902,17 +912,11 @@
             r.dkv[own * KU : own * KU + KU, :] += r.rdk[u].astype(F32)
 
     for i in range(8):
-        cols = slice(i * 128, i * 128 + 128)
-        r.sdkv[i] = r.dkv[cols, :].astype(BF)
-        grad = r.acct[:, cols].T * 0.125
-        r.sdq[i] = pack(grad).astype(BF)
-        r.dqb[cols, :] = (grad * keep_low).astype(BF)
+        r.sdkv[i] = r.dkv[i * 128 : i * 128 + 128, :].astype(BF)
     for mask in range(1, 8):
         device, to = peer(mask)
         send(r.sdkv.at[to], r.rdkv.at[p], r.dkv_s.at[mask], r.dkv_r.at[mask], device)
-        send(r.sdq.at[to], r.rdq.at[p], r.dq_s.at[mask], r.dq_r.at[mask], device)
     r.rdkv[p] = r.sdkv[p]
-    r.rdq[p] = r.sdq[p]
 
 
     fan_forward(r.gbp, r.gb_s, r.gb_r)
@@ -955,6 +959,8 @@
         send(r.spw.at[rows(to, 32)], r.rpw.at[p], r.pw_s.at[mask], r.pw_r.at[mask], device)
     r.rpw[p] = r.spw[rows(p, 32), :]
 
+    early = len(sends)
+
     ones = jnp.ones((128, 128), BF)
 
     def char_head_back(hh):
@@ -1057,6 +1063,28 @@
     r.rgn[p] = r.gn[...]
 
     final_cross(land["ffn"], FR // nz, r.fa_s, r.fa_r, r.xf_s, r.xf_r)
+    for copy in sends[:early]:
+        copy.wait_send()
+    del sends[:early]
+    for t in range(1, nz):
+        @pl.when(z + t < nz)
+        def _():
+            docs_copy(t, z).wait_send()
+
+    @pl.when(z + 1 < nz)
+    def _():
+        def sent(u, carry):
+            unit_copy(u).wait_send()
+            return carry
+
+        lax.fori_loop(0, 2 * z + 2, sent, 0)
+
+    def grads_sent(u, carry):
+        grad_copy(u).wait_send()
+        return carry
+
+    lax.fori_loop(jnp.maximum(2 * z - SLOTS, 0), 2 * z, grads_sent, 0)
+
     final_cross(land["att"], AR // nz, r.aa_s, r.aa_r, r.xa_s, r.xa_r)
     r.pfin[...] = planes_sum(r.zpw, r.pz_s, r.pz_r).astype(BF)
     for mask in range(1, 8):
@@ -1095,24 +1123,6 @@
             copy.wait()
     for copy in sends:
         copy.wait_send()
-    for t in range(1, nz):
-        @pl.when(z + t < nz)
-        def _():
-            docs_copy(t, z).wait_send()
-
-    @pl.when(z + 1 < nz)
-    def _():
-        def sent(u, carry):
-            unit_copy(u).wait_send()
-            return carry
-
-        lax.fori_loop(0, 2 * z + 2, sent, 0)
-
-    def grads_sent(u, carry):
-        grad_copy(u).wait_send()
-        return carry
-
-    lax.fori_loop(jnp.maximum(2 * z - SLOTS, 0), 2 * z, grads_sent, 0)
 
 
 def per_device(nz, *arguments):

time: 143 us -> 143 us (level)
  no operation moved by 1% of the time
where the time goes in v4:
time: 143 us; the launch traced here: 142 us
  Pallas kernels  142 us (99%)
    pallas_call x1, Pallas kernels, per_device(): pl.pallas_call(functools.partial(layer_kernel, nz, names), out_shape=out_...  138 us
    pallas_call x1, Pallas kernels, per_device(): pl.pallas_call(unpack_kernel, out_shape=grads, in_specs=[any_space] * len...  4.06 us

profile of v4, /device:TPU:12, one launch (start us, length us, event | category | flops | bytes accessed | tf_op | source)
XLA Modules:
  0.0 142.4 jit_solution(7948580368747783731)
XLA Ops:
  0.7 137.5 %shard_map.263 = (bf16[512,512]{1,0:T(8,128)(2,1)}, bf16[512,512]{1,0:T(8,128)(2,1)}, bf16[128,16,256]{2,1,0:T(8,128)(2,1)}, bf16[2,1024,256]{2,1,0:T(8,128)(2,1...) custom-call(bf16[512,512]{1,0:T(8,128)(2,1)} %refs_0_.1, ...), custom_call_target="tpu_custom_call" | custom-call | tf_op jit(solution)/shard_map/pallas_call | solution.py:1148
  138.2 4.1 %shard_map.264 = (bf16[512,512]{1,0:T(8,128)(2,1)}, bf16[512,512]{1,0:T(8,128)(2,1)}, bf16[128,16,256]{2,1,0:T(8,128)(2,1)}, f32[1,256]{1,0:T(1,128)}, f32[3,64,...) custom-call(bf16[512,512]{1,0:T(8,128)(2,1)} %get-tuple-element.36.r, ...), custom_call_target="tpu_custom_call" | custom-call | tf_op jit(solution)/shard_map/pallas_call | solution.py:1175
